TPU v7x, 256 devices: a whole 4x4x8 slice. The times are simulated.
256 devices in a mesh: pen: 32 (over z, y), slab: 8 (over x, core).
Axes of the slice: x: 4, y: 4, z: 8, core: 2. Of those that a mesh axis runs over, the one named last changes fastest.
Arguments:
- features: bfloat16 [524288, 128], P(('pen', 'slab')), may hold values from -6 to 6
- fractions: float32 [3, 524288], P(None, ('pen', 'slab')), may hold values from 0 to 1
- row_ids: int32 [256, 512], P(('pen', 'slab')), may hold values from -1 to 65535, as said below
- stencil_slots: int32 [16, 524288], P(None, ('pen', 'slab')), may hold values from 0 to 511, as said below
- stencil_z: int32 [524288], P(('pen', 'slab')), may hold values from 0 to 255
- atom_count: int32 [256], P(('pen', 'slab')), may hold values from 1 to 2048
- w_in: bfloat16 [128, 128], replicated, may hold values from -0.5 to 0.5
- w_out: float32 [128], replicated, may hold values from -0.5 to 0.5
Outputs:
- forces: float32 [3, 524288], P(None, ('pen', 'slab'))
- feature_grad: bfloat16 [524288, 128], P(('pen', 'slab'))
Inputs may be any that keep to these rules, and one draw needn't show every extreme that they name: `row_ids`: entries of a block's list are -1 or a row id x * 256 + y; the ids come first and are distinct within the block; at most 2 of one block's ids share both x mod 32 and y mod 8, and some block reaches that for every such pair. `stencil_slots`: entry 4 i + j of atom a names an id entry of the list of a's block, whose row is (x + i, y + j) modulo 256 for the atom's stencil corner (x, y).
All inputs are finite; a program needn't handle non-finite values.
Results may differ from a plain program's by a relative error of at most 0.0049.
Values sent between devices are 32-bit elements; how exact they have to be, the bound alone decides.
A program may use at most 64 MiB of HBM per device.

v0:
```python
import math

import jax
import jax.numpy as jnp
from jax import lax
from jax.sharding import PartitionSpec as P

GRID = 256
CAP_X = 1
CAP_Y = 2


COUPLE = 8.0
SMOOTH = 1.0


def spline_weights(fraction):
    rest = 1.0 - fraction
    square = fraction * fraction
    cube = square * fraction
    values = jnp.stack(
        [
            rest * rest * rest / 6.0,
            (3.0 * cube - 6.0 * square + 4.0) / 6.0,
            (-3.0 * cube + 3.0 * square + 3.0 * fraction + 1.0) / 6.0,
            cube / 6.0,
        ]
    )
    slopes = jnp.stack(
        [
            -rest * rest / 2.0,
            (3.0 * square - 4.0 * fraction) / 2.0,
            (-3.0 * square + 2.0 * fraction + 1.0) / 2.0,
            square / 2.0,
        ]
    )
    return (values, slopes)


def kernel_values(wave_a, wave_b, wave_c, grid_size):
    squared = (wave_a * wave_a + wave_b * wave_b + wave_c * wave_c).astype(jnp.float32)
    midpoint = grid_size // 2
    nyquist = (
        (jnp.abs(wave_a) == midpoint)
        | (jnp.abs(wave_b) == midpoint)
        | (jnp.abs(wave_c) == midpoint)
    )
    safe = jnp.maximum(squared, 1.0)
    damped = jnp.exp(-((SMOOTH * math.pi / grid_size) ** 2) * squared)
    values = COUPLE * damped * (grid_size * grid_size) / (4.0 * math.pi * math.pi * safe)
    return jnp.where((squared > 0) & jnp.logical_not(nyquist), values, 0.0)


def signed_index(index, grid_size):
    return jnp.where(index < grid_size // 2, index, index - grid_size)


def charge_head(features, w_in, w_out):
    hidden_pre = jnp.dot(features, w_in, preferred_element_type=jnp.float32)
    sigma = jax.nn.sigmoid(hidden_pre)
    charges = jnp.dot(hidden_pre * sigma, w_out, precision=lax.Precision.HIGHEST)
    lifted = (sigma * (1.0 + hidden_pre * (1.0 - sigma)) * w_out).astype(jnp.bfloat16)
    direction = lax.dot_general(
        lifted, w_in, (((1,), (1,)), ((), ())), preferred_element_type=jnp.float32
    )
    return (charges, direction)


def contract(left, right, left_dim, right_dim):
    return lax.dot_general(
        left,
        right,
        (((left_dim,), (right_dim,)), ((), ())),
        precision=lax.Precision.HIGHEST,
        preferred_element_type=jnp.float32,
    )


def phase_tables(ordering, wave_count, grid_size):
    frequency = jnp.arange(wave_count, dtype=jnp.int32)
    phases = ordering[:, None] * frequency[None, :] % grid_size
    angles = phases.astype(jnp.float32) * (2.0 * math.pi / grid_size)
    return (jnp.cos(angles), jnp.sin(angles))


def gathered_order(group_count, grid_size):
    position = jnp.arange(grid_size, dtype=jnp.int32)
    local_size = grid_size // group_count
    return position // local_size + group_count * (position % local_size)


def forward_pair(real_part, imag_part, cosine, sine):
    return (
        contract(real_part, cosine, 0, 0) + contract(imag_part, sine, 0, 0),
        contract(imag_part, cosine, 0, 0) - contract(real_part, sine, 0, 0),
    )


def inverse_pair(real_part, imag_part, cosine, sine):
    return (
        contract(cosine, real_part, 1, 1) - contract(sine, imag_part, 1, 1),
        contract(cosine, imag_part, 1, 1) + contract(sine, real_part, 1, 1),
    )


def solve_pencil(
    pencil,
    first_out,
    second_out,
    second_back,
    first_back,
    count_one,
    count_two,
    index_one,
    index_two,
):
    grid_size = GRID
    wave_count = grid_size // 2
    local_one = grid_size // count_one
    local_two = grid_size // count_two
    wave_local = wave_count // count_one
    natural = jnp.arange(grid_size, dtype=jnp.int32)
    z_cosine, z_sine = phase_tables(natural, wave_count, grid_size)
    real_part = contract(pencil, z_cosine, 1, 0)
    imag_part = -contract(pencil, z_sine, 1, 0)
    stacked = jnp.stack([real_part, imag_part]).reshape(
        2, local_one, local_two, count_one, wave_local
    )
    arrived = first_out(stacked).reshape(2, grid_size, local_two * wave_local)
    one_cosine, one_sine = phase_tables(gathered_order(count_one, grid_size), grid_size, grid_size)
    real_part, imag_part = forward_pair(arrived[0], arrived[1], one_cosine, one_sine)
    stacked = jnp.stack([real_part, imag_part]).reshape(
        2, local_two, wave_local, count_two, local_two
    )
    arrived = second_out(stacked).reshape(2, grid_size, wave_local * local_two)
    two_cosine, two_sine = phase_tables(gathered_order(count_two, grid_size), grid_size, grid_size)
    real_part, imag_part = forward_pair(arrived[0], arrived[1], two_cosine, two_sine)
    wave_one = signed_index(
        index_one * wave_local + jnp.arange(wave_local, dtype=jnp.int32), grid_size
    )
    wave_two = signed_index(
        index_two * local_two + jnp.arange(local_two, dtype=jnp.int32), grid_size
    )
    wave_three = signed_index(natural, grid_size)
    kernel = kernel_values(
        wave_one[:, None, None], wave_two[None, :, None], wave_three[None, None, :], grid_size
    )
    kernel = (kernel * (1.0 / grid_size**3)).reshape(wave_local * local_two, grid_size)
    real_part = real_part * kernel
    imag_part = imag_part * kernel
    real_part, imag_part = inverse_pair(real_part, imag_part, two_cosine, two_sine)
    arrived = second_back(
        jnp.stack([real_part, imag_part]).reshape(2, grid_size, wave_local, 1, local_two)
    )
    arrived = arrived.reshape(2, local_two * wave_local, grid_size)
    real_part, imag_part = inverse_pair(arrived[0], arrived[1], one_cosine, one_sine)
    arrived = first_back(
        jnp.stack([real_part, imag_part]).reshape(2, grid_size, local_two, 1, wave_local)
    )
    arrived = arrived.reshape(2, local_one * local_two, wave_count)
    weighting = jnp.where(jnp.arange(wave_count, dtype=jnp.int32) == 0, 1.0, 2.0)
    return contract(arrived[0] * weighting, z_cosine, 1, 1) - contract(
        arrived[1] * weighting, z_sine, 1, 1
    )


def local(features, fractions, row_ids, stencil_slots, stencil_z, atom_count, w_in, w_out):
    count_pen = lax.axis_size("pen")
    count_slab = lax.axis_size("slab")
    devices = count_pen * count_slab
    capacity = CAP_X * CAP_Y
    atom_dev = features.shape[0]
    rows_dev = row_ids.shape[1]
    live = jnp.arange(atom_dev, dtype=jnp.int32) < atom_count[0]
    charges, direction = charge_head(features, w_in, w_out)
    charges = jnp.where(live, charges, 0.0)
    weight_x, slope_x = spline_weights(fractions[0])
    weight_y, slope_y = spline_weights(fractions[1])
    weight_z, slope_z = spline_weights(fractions[2])
    row_slots = stencil_slots.reshape(4, 4, atom_dev)
    z_cells = (stencil_z[None, :] + jnp.arange(4, dtype=jnp.int32)[:, None]) % GRID
    slot_index = jnp.broadcast_to(row_slots[:, :, None, :], (4, 4, 4, atom_dev))
    z_index = jnp.broadcast_to(z_cells[None, None, :, :], (4, 4, 4, atom_dev))
    amounts = (
        charges[None, None, None, :]
        * weight_x[:, None, None, :]
        * weight_y[None, :, None, :]
        * weight_z[None, None, :, :]
    )
    block_rows = jnp.zeros((rows_dev, GRID), jnp.float32).at[slot_index, z_index].add(amounts)
    row_list = row_ids[0]
    in_use = row_list >= 0
    safe_rows = jnp.maximum(row_list, 0)
    x_cell = safe_rows // GRID
    y_cell = safe_rows % GRID
    owner_rank = x_cell % count_pen * count_slab + y_cell % count_slab
    matches = (
        (owner_rank[:, None] == jnp.arange(devices, dtype=jnp.int32)[None, :]) & in_use[:, None]
    ).astype(jnp.int32)
    position = jnp.sum((jnp.cumsum(matches, axis=0) - matches) * matches, axis=1)
    target_slot = jnp.where(in_use, owner_rank * capacity + position, devices * capacity)
    x_local = x_cell // count_pen
    y_local = y_cell // count_slab
    cells_x = GRID // count_pen
    cells_y = GRID // count_slab
    local_label = y_local * cells_x + x_local
    outgoing = (
        jnp.zeros((devices * capacity, GRID), jnp.float32)
        .at[target_slot]
        .set(block_rows, mode="drop")
    )
    labels = (
        jnp.full((devices * capacity,), -1, jnp.int32).at[target_slot].set(local_label, mode="drop")
    )
    arrived_rows, arrived_labels = (
        lax.all_to_all(
            lax.all_to_all(
                outgoing.reshape(count_pen, count_slab, capacity, GRID),
                "pen",
                split_axis=0,
                concat_axis=0,
                tiled=True,
            ),
            "slab",
            split_axis=1,
            concat_axis=1,
            tiled=True,
        ),
        lax.all_to_all(
            lax.all_to_all(
                labels.reshape(count_pen, count_slab, capacity),
                "pen",
                split_axis=0,
                concat_axis=0,
                tiled=True,
            ),
            "slab",
            split_axis=1,
            concat_axis=1,
            tiled=True,
        ),
    )
    cell_count = cells_x * cells_y
    flat_labels = arrived_labels.reshape(-1)
    flat_rows = arrived_rows.reshape(-1, GRID)
    pencil = (
        jnp.zeros((cell_count, GRID), jnp.float32)
        .at[jnp.where(flat_labels >= 0, flat_labels, cell_count)]
        .add(flat_rows, mode="drop")
    )

    def first_out(value):
        return lax.all_to_all(value, "slab", split_axis=3, concat_axis=1, tiled=True)

    def second_out(value):
        return lax.all_to_all(value, "pen", split_axis=3, concat_axis=1, tiled=True)

    def second_back(value):
        return lax.all_to_all(value, "pen", split_axis=1, concat_axis=3, tiled=True)

    def first_back(value):
        return lax.all_to_all(value, "slab", split_axis=1, concat_axis=3, tiled=True)

    field = solve_pencil(
        pencil,
        first_out,
        second_out,
        second_back,
        first_back,
        count_slab,
        count_pen,
        lax.axis_index("slab"),
        lax.axis_index("pen"),
    )
    replies = jnp.where((flat_labels >= 0)[:, None], field[jnp.maximum(flat_labels, 0)], 0.0)
    returned = lax.all_to_all(
        lax.all_to_all(
            replies.reshape(count_pen, count_slab, capacity, GRID),
            "pen",
            split_axis=0,
            concat_axis=0,
            tiled=True,
        ),
        "slab",
        split_axis=1,
        concat_axis=1,
        tiled=True,
    ).reshape(-1, GRID)
    row_field = returned[jnp.minimum(target_slot, devices * capacity - 1)]
    samples = row_field[slot_index, z_index]
    potential = jnp.sum(
        weight_x[:, None, None, :]
        * weight_y[None, :, None, :]
        * weight_z[None, None, :, :]
        * samples,
        axis=(0, 1, 2),
    )
    grad_x = jnp.sum(
        slope_x[:, None, None, :]
        * weight_y[None, :, None, :]
        * weight_z[None, None, :, :]
        * samples,
        axis=(0, 1, 2),
    )
    grad_y = jnp.sum(
        weight_x[:, None, None, :]
        * slope_y[None, :, None, :]
        * weight_z[None, None, :, :]
        * samples,
        axis=(0, 1, 2),
    )
    grad_z = jnp.sum(
        weight_x[:, None, None, :]
        * weight_y[None, :, None, :]
        * slope_z[None, None, :, :]
        * samples,
        axis=(0, 1, 2),
    )
    forces = -charges[None, :] * jnp.stack([grad_x, grad_y, grad_z])
    feature_grad = jnp.where(live[:, None], potential[:, None] * direction, 0.0).astype(
        jnp.bfloat16
    )
    return (forces, feature_grad)


def solution(mesh):
    placed = (
        P(("pen", "slab"), None),
        P(None, ("pen", "slab")),
        P(("pen", "slab"), None),
        P(None, ("pen", "slab")),
        P(("pen", "slab")),
        P(("pen", "slab")),
        P(),
        P(),
    )
    return jax.shard_map(
        local,
        mesh=mesh,
        in_specs=placed,
        out_specs=(P(None, ("pen", "slab")), P(("pen", "slab"), None)),
        check_vma=False,
    )
```

profile of v0, /device:TPU:1, one launch (start us, length us, event | category | flops | bytes accessed | tf_op | source)
XLA Modules:
  0.0 2180.4 jit_solution(548322528872740340)
XLA Ops:
  3.4 2.4 scatter_custom_fusion
  6.8 12.0 all-to-all-start
  26.6 682.7 %scatter_custom_fusion.3 = f32[131072]{0:T(1024)S(1)} fusion(s32[131072]{0:T(1024)S(1)} %bitcast.175, f32[131072]{0:T(1024)S(1)} %bitcast.174, f32[]{:T(128)} %constant.218.clone.1), kind=kCustom, calls=%fused_computation.63 | custom fusion | flops 131072 | bytes 524292
  709.5 2.4 scatter_custom_fusion.1
  713.0 225.7 %all-to-all-start.2 = ((f32[32,8,2,256]{3,2,1,0:T(2,128)}), f32[32,8,2,256]{3,2,1,0:T(2,128)S(1)}, u32[]{:S(2)}, u32[]{:S(2)}) async-start(f32[32,8,2,256]{3,2,1,0:T(2,128)} %reshape.618), calls=%async_computation.2 | async-start | bytes 1048576 | tf_op jit(solution)/shard_map/all_to_all | solution.py:217
  939.4 12.0 all-to-all-done.2
  951.4 5.2 all-to-all-start.1
  957.5 3.6 all-to-all-done.1
  961.2 4.6 all-to-all-start.3
  966.1 9.2 all-to-all-done.3
  975.9 3.4 scatter_custom_fusion.2
  986.4 4.4 all-to-all-start.4
  990.9 6.3 all-to-all-done.4
  1010.7 4.5 all-to-all-start.5
  1015.8 9.5 all-to-all-done.5
  1028.7 1.9 copy.177
  1049.4 5.4 all-to-all-start.6
  1054.8 10.4 all-to-all-done.6
  1079.0 7.3 all-to-all-start.7
  1086.5 6.3 all-to-all-done.7
  1102.5 18.4 all_to_all.90
  1121.9 6.9 all-to-all-start.9
  1129.4 8.9 all-to-all-done.9
  1140.6 1036.4 %gather_fusion.2 = f32[131072]{0:T(1024)S(1)} fusion(f32[512,256]{1,0:T(8,128)S(1)} %gather_fusion.1, s32[131072]{0:T(1024)S(1)} %bitcast.163), kind=kCustom, calls=%fused_computation.2 | custom fusion | bytes 2097152 | tf_op jit(solution)/shard_map/gather | solution.py:290
  (201 shorter events, 87.8 us)
Async XLA Ops:
  0.6 21.7 copy-start
  0.7 18.2 copy-start.12
  0.7 18.5 copy-start.10
  2.7 16.6 copy-start.15
  3.0 18.4 copy-start.20
  6.8 706.1 %all-to-all-start = ((s32[32,8,2]{1,2,0:T(2,128)}), s32[32,8,2]{1,2,0:T(2,128)S(1)}, u32[]{:S(2)}, u32[]{:S(2)}) async-start(s32[32,8,2]{1,2,0:T(2,128)} %copy.164), calls=%async_computation | async-start | bytes 65536 | tf_op jit(solution)/shard_map/all_to_all | solution.py:230
  713.0 238.4 %all-to-all-start.2 = ((f32[32,8,2,256]{3,2,1,0:T(2,128)}), f32[32,8,2,256]{3,2,1,0:T(2,128)S(1)}, u32[]{:S(2)}, u32[]{:S(2)}) async-start(f32[32,8,2,256]{3,2,1,0:T(2,128)} %reshape.618), calls=%async_computation.2 | async-start | bytes 1048576 | tf_op jit(solution)/shard_map/all_to_all | solution.py:217
  951.4 9.8 all-to-all-start.1
  961.2 14.1 all-to-all-start.3
  986.4 10.9 all-to-all-start.4
  1010.7 14.5 all-to-all-start.5
  1049.4 15.8 all-to-all-start.6
  1079.0 13.8 all-to-all-start.7
  1102.1 26.6 %copy-start.2 = (s32[4,4,4,2048,1]{3,2,1,0,4:T(4,128)S(1)}, s32[4,4,4,2048,1]{3,2,1,0,4:T(4,128)}, u32[]{:S(2)}) copy-start(s32[4,4,4,2048,1]{3,2,1,0,4:T(4,128)} %get-tuple-element.20) | copy-start | bytes 1572868
  1121.9 16.4 all-to-all-start.9
  1140.5 1036.7 %copy-start.5 = (f32[4,4,2048]{2,1,0:T(4,128)S(1)}, f32[4,4,2048]{2,1,0:T(4,128)}, u32[]{:S(2)}) copy-start(f32[4,4,2048]{2,1,0:T(4,128)} %get-tuple-element.23) | copy-start | bytes 393220
  1140.5 1036.7 %copy-start.6 = (f32[4,4,2048]{2,1,0:T(4,128)S(1)}, f32[4,4,2048]{2,1,0:T(4,128)}, u32[]{:S(2)}) copy-start(f32[4,4,2048]{2,1,0:T(4,128)} %get-tuple-element.25) | copy-start | bytes 393220
  1140.5 1036.7 %copy-start.7 = (f32[4,4,2048]{2,1,0:T(4,128)S(1)}, f32[4,4,2048]{2,1,0:T(4,128)}, u32[]{:S(2)}) copy-start(f32[4,4,2048]{2,1,0:T(4,128)} %get-tuple-element.26) | copy-start | bytes 393220
  1140.5 1036.7 %copy-start.9 = (f32[4,2048]{1,0:T(4,128)S(1)}, f32[4,2048]{1,0:T(4,128)}, u32[]{:S(2)}) copy-start(f32[4,2048]{1,0:T(4,128)} %copy-done.8) | copy-start | bytes 98308
  1140.5 1036.7 %copy-start.11 = (f32[4,2048]{1,0:T(4,128)S(1)}, f32[4,2048]{1,0:T(4,128)}, u32[]{:S(2)}) copy-start(f32[4,2048]{1,0:T(4,128)} %get-tuple-element.65) | copy-start | bytes 98308
  1140.5 1037.3 %copy-start.4 = (f32[2048,128]{1,0:T(8,128)S(1)}, f32[2048,128]{1,0:T(8,128)}, u32[]{:S(2)}) copy-start(f32[2048,128]{1,0:T(8,128)} %copy-done.3) | copy-start | bytes 3145732
  1140.5 1037.3 %copy-start.14 = (bf16[128,128]{1,0:T(8,128)(2,1)S(1)}, bf16[128,128]{1,0:T(8,128)(2,1)}, u32[]{:S(2)}) copy-start(bf16[128,128]{1,0:T(8,128)(2,1)} %param.14) | copy-start | bytes 98308
  1140.6 1037.3 %copy-start.18 = (pred[2048]{0:T(1024)(128)(4,1)S(1)}, pred[2048]{0:T(1024)(128)(4,1)}, u32[]{:S(2)}) copy-start(pred[2048]{0:T(1024)(128)(4,1)} %iota_compare_fusion.2) | copy-start | bytes 6148
  1140.6 1037.3 %copy-start.22 = (f32[128]{0:T(128)S(1)}, f32[128]{0:T(128)}, u32[]{:S(2)}) copy-start(f32[128]{0:T(128)} %param.15) | copy-start | bytes 1540
  (8 other events, 14.8 us)
where the time goes:
time: 2190 us; the launch traced here: 2180 us
  local copies, waits for them, and re-layouts  1080 us (49%)
  other arithmetic  707 us (32%)
  starting transfers between devices  276 us (13%)
  waiting for transfers between devices  66.2 us (3%)
  matrix products  28.7 us (1%)
    gather x2, local copies, waits for them, and re-layouts, local(): samples = row_field[slot_index, z_index]  1040 us
    unnamed x7, other arithmetic  688 us
    all_to_all x1, starting transfers between devices, local(): lax.all_to_all(outgoing.reshape(count_pen, count_slab, capacity, GRID), '...  226 us
  transfers between devices with their start and end apart: 9, of which 8 were waited for; matrix products, arithmetic and copies ran while one was open for 32% of the time, Pallas kernels for 0%

commit v1 on v0

v1 whole, which is shorter than its diff:
```python
import functools
import math

import jax
import jax.numpy as jnp
import ml_dtypes
import numpy as np
from jax import lax
from jax.experimental import pallas as pl
from jax.experimental.pallas import tpu as pltpu
from jax.sharding import PartitionSpec as P

GRID = 256
COUPLE = 8.0
SMOOTH = 1.0
ROWS = 512
ATOMS = 2048
DEVICES = 256
CHUNK = 512
VMEM_LIMIT = 56 * 1024 * 1024
F32 = jnp.float32
BF16 = jnp.bfloat16

NN = (((1,), (0,)), ((), ()))
NT = (((1,), (1,)), ((), ()))


def dot(left, right, dims=NN):
    return lax.dot_general(left, right, dims, preferred_element_type=F32)


def split(value):
    high = value.astype(BF16)
    low = (value - high.astype(F32)).astype(BF16)
    return (high, low)


def dot3(left, right, dims=NN):
    return (
        dot(left[0], right[0], dims)
        + dot(left[0], right[1], dims)
        + dot(left[1], right[0], dims)
    )


def fourier_basis():
    cell = np.arange(GRID)
    wave = np.arange(GRID)
    wave = np.where(wave <= GRID // 2, wave, wave - GRID // 2)
    angle = 2.0 * np.pi * ((wave[:, None] * cell[None, :]) % GRID) / GRID
    basis = np.where(np.arange(GRID)[:, None] <= GRID // 2, np.cos(angle), np.sin(angle))
    scale = np.where((np.arange(GRID) == 0) | (np.arange(GRID) == GRID // 2), 1.0, 2.0)
    return basis * np.sqrt(scale / GRID)[:, None]


def split_table(table):
    table = table.astype(np.float32)
    high = table.astype(ml_dtypes.bfloat16)
    low = (table - high.astype(np.float32)).astype(ml_dtypes.bfloat16)
    return [high, low]


def tables():
    basis = fourier_basis()
    place = np.arange(GRID)
    along_x = basis[:, (place % 8) * 32 + place // 8]
    along_y = basis[:, (place % 32) * 8 + place // 32]
    plane = np.stack(split_table(along_x) + split_table(along_x.T) + split_table(along_y))
    return (np.stack(split_table(basis)), np.stack(split_table(basis.T)), plane)


def spline_values(u):
    rest = 1.0 - u
    square = u * u
    cube = square * u
    return (
        rest * rest * rest / 6.0,
        (3.0 * cube - 6.0 * square + 4.0) / 6.0,
        (-3.0 * cube + 3.0 * square + 3.0 * u + 1.0) / 6.0,
        cube / 6.0,
    )


def spline_slopes(u):
    rest = 1.0 - u
    square = u * u
    return (
        -rest * rest / 2.0,
        (3.0 * square - 4.0 * u) / 2.0,
        (-3.0 * square + 2.0 * u + 1.0) / 2.0,
        square / 2.0,
    )


def pick(step, values):
    out = jnp.where(step == 3, values[3], 0.0)
    for k in (2, 1, 0):
        out = jnp.where(step == k, values[k], out)
    return out


def row_to_columns(row):
    return jnp.transpose(jnp.broadcast_to(row, (128, 128)))


def bin_labels(row_ids, ids_cols, bins_cols):
    ids = row_ids[...]
    used = ids >= 0
    x = ids >> 8
    y = ids & 255
    group = jnp.where(used, (x & 31) * 8 + (y & 7), -1)
    label = ((x >> 5) * 32 + (y >> 3)).astype(F32)
    group_f = group.astype(F32)
    place = lax.broadcasted_iota(jnp.int32, (128, ROWS), 1)
    row = lax.broadcasted_iota(jnp.int32, (128, ROWS), 0)
    rank = jnp.zeros((1, ROWS), F32)
    for c in range(ROWS // 128):
        lanes = slice(c * 128, (c + 1) * 128)
        ids_cols[lanes, :] = row_to_columns(ids[:, lanes].astype(F32))
        column = row_to_columns(group_f[:, lanes])
        column = jnp.concatenate([column] * (ROWS // 128), axis=1)
        same = (column == group_f) & (row + c * 128 < place)
        rank += jnp.sum(jnp.where(same, 1.0, 0.0), axis=0, keepdims=True)
    target = jnp.where(used, rank.astype(jnp.int32) * 256 + group, -1)
    for c in range(ROWS // 128):
        hit = target == row + c * 128
        value = jnp.sum(jnp.where(hit, label + 1.0, 0.0), axis=1, keepdims=True) - 1.0
        bins_cols[c * 128 : (c + 1) * 128, :] = jnp.broadcast_to(value, (128, 128))


def corners(slots, ids_cols, corner):
    row = lax.broadcasted_iota(jnp.int32, (ROWS, 128), 0)
    for c in range(ATOMS // 128):
        lanes = slice(c * 128, (c + 1) * 128)
        hit = slots[0:1, lanes] == row
        value = jnp.sum(jnp.where(hit, ids_cols[...], 0.0), axis=0, keepdims=True)
        corner[0:1, lanes] = value.astype(jnp.int32)


def class_weights(corner, fractions, tab_x, tab_y, slopes):
    x0 = corner[0:1, :] >> 8
    y0 = corner[0:1, :] & 255
    value_x = spline_values(fractions[0:1, :])
    value_y = spline_values(fractions[1:2, :])
    step_y = (lax.broadcasted_iota(jnp.int32, (8, ATOMS), 0) - y0) & 7
    tab_y[0:8, :] = pick(step_y, value_y)
    tab_y[8:16, :] = ((((y0 + step_y) >> 3) & 31)).astype(F32)
    if slopes:
        slope_x = spline_slopes(fractions[0:1, :])
        slope_y = spline_slopes(fractions[1:2, :])
        tab_y[16:24, :] = pick(step_y, slope_y)
    for b in range(4):
        rows = slice(b * 8, (b + 1) * 8)
        step_x = (lax.broadcasted_iota(jnp.int32, (8, ATOMS), 0) + b * 8 - x0) & 31
        tab_x[0, rows, :] = pick(step_x, value_x)
        tab_x[1, rows, :] = ((((x0 + step_x) >> 5) & 7) * 32).astype(F32)
        if slopes:
            tab_x[2, rows, :] = pick(step_x, slope_x)


def class_weights_z(stencil_z, fractions, tab_z, slopes):
    z0 = stencil_z[0:1, :]
    step_z = (lax.broadcasted_iota(jnp.int32, (8, ATOMS), 0) - z0) & 7
    tab_z[0:8, :] = pick(step_z, spline_values(fractions[2:3, :]))
    tab_z[8:16, :] = ((((z0 + step_z) >> 3) & 31)).astype(F32)
    if slopes:
        tab_z[16:24, :] = pick(step_z, spline_slopes(fractions[2:3, :]))


def row_weights(tab_x, tab_y, bins_cols, lanes, outs, kinds):
    def twice(part):
        return jnp.concatenate([part, part], axis=0)

    wy = twice(tab_y[0:8, lanes])
    ky = twice(tab_y[8:16, lanes])
    sy = twice(tab_y[16:24, lanes]) if kinds > 1 else None
    width = wy.shape[1]

    def pair(index, i):
        rows = [tab_x[index, pl.ds(2 * i + k, 1), lanes] for k in range(2)]
        return jnp.concatenate([jnp.broadcast_to(row, (8, width)) for row in rows], axis=0)

    @pl.loop(0, 16)
    def _(i):
        wx = pair(0, i)
        key = pair(1, i) + ky
        values = [wx * wy]
        if kinds > 1:
            values += [pair(2, i) * wy, wx * sy]
        for rank in range(2):
            rows = pl.ds(pl.multiple_of(rank * 256 + i * 16, 16), 16)
            label = bins_cols[rows, :]
            label = jnp.concatenate([label] * (width // 128), axis=1)
            hit = key == label
            for k, value in enumerate(values):
                high, low = split(jnp.where(hit, value, 0.0))
                outs[2 * k][rows, :] = high
                outs[2 * k + 1][rows, :] = low


def hidden(features, w_in, w_out, lanes):
    w_in_t = jnp.transpose(w_in[...].astype(F32)).astype(BF16)
    pre = dot(w_in_t, features[lanes, :], NT)
    sigma = jax.nn.sigmoid(pre)
    out_w = row_to_columns(w_out[...])
    out_w = jnp.concatenate([out_w] * (pre.shape[1] // 128), axis=1)
    return (pre, sigma, out_w)


def spread_kernel(
    row_ids,
    slots,
    stencil_z,
    fractions,
    atom_count,
    features,
    w_in,
    w_out,
    basis,
    sent,
    labels,
    bins_cols,
    charges,
    corner,
    ids_cols,
    tab_x,
    tab_y,
    tab_z,
    high,
    low,
    z_high,
    z_low,
    mesh_rows,
):
    bin_labels(row_ids, ids_cols, bins_cols)
    for c in range(ROWS // 128):
        part = jnp.transpose(bins_cols[c * 128 : (c + 1) * 128, :])
        labels[0:1, c * 128 : (c + 1) * 128] = part[0:1, :]
    corners(slots, ids_cols, corner)
    for c in range(ATOMS // CHUNK):
        lanes = slice(c * CHUNK, (c + 1) * CHUNK)
        pre, sigma, out_w = hidden(features, w_in, w_out, lanes)
        charge = jnp.sum(pre * sigma * out_w, axis=0, keepdims=True)
        atom = lax.broadcasted_iota(jnp.int32, (1, CHUNK), 1) + c * CHUNK
        charges[0:1, lanes] = jnp.where(atom < atom_count[0], charge, 0.0)
    class_weights(corner, fractions, tab_x, tab_y, False)
    class_weights_z(stencil_z, fractions, tab_z, False)
    for c in range(ATOMS // CHUNK):
        lanes = slice(c * CHUNK, (c + 1) * CHUNK)
        row_weights(tab_x, tab_y, bins_cols, lanes, [high, low], 1)
        key = tab_z[8:16, lanes]
        amount = tab_z[0:8, lanes] * charges[0:1, lanes]
        amount_high = amount.astype(BF16).astype(F32)
        amount_low = amount - amount_high
        for h in range(0, 32, 2):
            rows = slice(h * 8, h * 8 + 16)
            hits = (key == float(h), key == float(h + 1))
            z_high[rows, :] = jnp.concatenate(
                [jnp.where(hit, amount_high, 0.0) for hit in hits], axis=0
            ).astype(BF16)
            z_low[rows, :] = jnp.concatenate(
                [jnp.where(hit, amount_low, 0.0) for hit in hits], axis=0
            ).astype(BF16)
        total = dot3((z_high[...], z_low[...]), (high[...], low[...]), NT)
        if c == 0:
            mesh_rows[...] = total
        else:
            mesh_rows[...] += total
    sent[...] = dot3((basis[0], basis[1]), split(mesh_rows[...]))


def solve_kernel(rows, labels, tabs, out, rows_t, labels_t, plane, replies):
    for b in range(2):
        for c in range(ROWS // 128):
            src = (slice(b * 128, (b + 1) * 128), slice(c * 128, (c + 1) * 128))
            dst = (slice(c * 128, (c + 1) * 128), slice(b * 128, (b + 1) * 128))
            rows_t[dst] = jnp.transpose(rows[src])
            labels_t[dst] = jnp.transpose(labels[src])
    lane_class = lax.broadcasted_iota(jnp.int32, (8, GRID), 0).astype(F32)
    cell_y = lax.broadcasted_iota(jnp.int32, (32, GRID), 0).astype(F32)

    @pl.loop(0, 32)
    def _(xb):
        groups = []
        for rank in range(2):
            at = pl.ds(pl.multiple_of(rank * 256 + xb * 8, 8), 8)
            value = rows_t[at, :]
            value_high = value.astype(BF16).astype(F32)
            label = labels_t[at, :]
            label_x = jnp.floor(label * (1.0 / 32.0))
            groups.append((value_high, value - value_high, label_x, label - 32.0 * label_x))
        pieces = []
        for yb in range(8):
            left, right = [], []
            for value_high, value_low, label_x, label_y in groups:
                hit = jnp.broadcast_to(label_x[yb : yb + 1], (8, GRID)) == lane_class
                both = [
                    jnp.where(hit, jnp.broadcast_to(part[yb : yb + 1], (8, GRID)), 0.0)
                    for part in (value_high, value_low)
                ]
                left.append(jnp.concatenate(both, axis=0).astype(BF16))
                hit = jnp.broadcast_to(label_y[yb : yb + 1], (32, GRID)) == cell_y
                right.append(jnp.where(hit, 1.0, 0.0).astype(BF16))
            piece = dot(jnp.concatenate(left, axis=1), jnp.concatenate(right, axis=1), NT)
            pieces.append(piece[0:8] + piece[8:16])
        plane[pl.ds(pl.multiple_of(xb * 8, 8), 8), :] = jnp.concatenate(pieces, axis=1)

    along_x, back_x, along_y = [(tabs[2 * k], tabs[2 * k + 1]) for k in range(3)]
    spectrum = dot3(along_x, split(plane[...]))
    spectrum = dot3(split(spectrum), along_y, NT)
    half = GRID // 2
    device = lax.axis_index("pen") * lax.axis_size("slab") + lax.axis_index("slab")

    def wave(index):
        return jnp.where(index <= half, index, index - half)

    wave_x = wave(lax.broadcasted_iota(jnp.int32, (GRID, GRID), 0))
    wave_y = wave(lax.broadcasted_iota(jnp.int32, (GRID, GRID), 1))
    wave_z = wave(device)
    squared = (wave_x * wave_x + wave_y * wave_y + wave_z * wave_z).astype(F32)
    damped = jnp.exp(-((SMOOTH * math.pi / GRID) ** 2) * squared)
    values = COUPLE * damped * (GRID * GRID) / (4.0 * math.pi * math.pi * jnp.maximum(squared, 1.0))
    keep = (squared > 0) & (wave_x != half) & (wave_y != half) & (wave_z != half)
    spectrum = spectrum * jnp.where(keep, values, 0.0)
    field = dot3(back_x, split(spectrum))
    plane[...] = dot3(split(field), along_y)

    upper = lax.broadcasted_iota(jnp.int32, (8, 128), 0) >= 4
    offset = (lax.broadcasted_iota(jnp.int32, (8, 128), 0) & 3) * 32

    @pl.loop(0, 32)
    def _(xb):
        sources = []
        field_rows = plane[pl.ds(pl.multiple_of(xb * 8, 8), 8), :]
        for h in range(8):
            row = jnp.broadcast_to(field_rows[h : h + 1], (8, GRID))
            sources.append(jnp.where(upper, row[:, 128:], row[:, :128]))
        for rank in range(2):
            at = pl.ds(pl.multiple_of(rank * 256 + xb * 8, 8), 8)
            for b in range(2):
                label = labels_t[at, b * 128 : (b + 1) * 128].astype(jnp.int32)
                label_x = label >> 5
                index = (label & 31) + offset
                value = jnp.zeros((8, 128), F32)
                for h in range(8):
                    taken = jnp.take_along_axis(
                        sources[h], index, axis=1, mode="promise_in_bounds"
                    )
                    value = jnp.where(label_x == h, taken, value)
                replies[at, b * 128 : (b + 1) * 128] = value

    for b in range(2):
        for c in range(ROWS // 128):
            src = (slice(c * 128, (c + 1) * 128), slice(b * 128, (b + 1) * 128))
            dst = (slice(b * 128, (b + 1) * 128), slice(c * 128, (c + 1) * 128))
            out[dst] = jnp.transpose(replies[src])


def sample_kernel(
    returned,
    corner,
    charges,
    bins_cols,
    stencil_z,
    fractions,
    atom_count,
    features,
    w_in,
    w_out,
    basis_t,
    forces,
    grads,
    tab_x,
    tab_y,
    tab_z,
    field_high,
    field_low,
    *weights,
):
    class_weights(corner, fractions, tab_x, tab_y, True)
    class_weights_z(stencil_z, fractions, tab_z, True)
    field_high[...], field_low[...] = split(
        dot3((basis_t[0], basis_t[1]), split(returned[...]))
    )
    for c in range(ATOMS // CHUNK):
        lanes = slice(c * CHUNK, (c + 1) * CHUNK)
        row_weights(tab_x, tab_y, bins_cols, lanes, weights, 3)
        key = tab_z[8:16, lanes]
        sums = []
        for k in range(3):
            total = dot3(
                (field_high[...], field_low[...]), (weights[2 * k][...], weights[2 * k + 1][...])
            )
            chosen = jnp.zeros((8, CHUNK), F32)
            for h in range(32):
                chosen = jnp.where(key == float(h), total[h * 8 : (h + 1) * 8], chosen)
            sums.append(chosen)
        wz = tab_z[0:8, lanes]
        potential = jnp.sum(wz * sums[0], axis=0, keepdims=True)
        charge = -charges[0:1, lanes]
        forces[0:1, lanes] = charge * jnp.sum(wz * sums[1], axis=0, keepdims=True)
        forces[1:2, lanes] = charge * jnp.sum(wz * sums[2], axis=0, keepdims=True)
        forces[2:3, lanes] = charge * jnp.sum(tab_z[16:24, lanes] * sums[0], axis=0, keepdims=True)
        atom = lax.broadcasted_iota(jnp.int32, (1, CHUNK), 1) + c * CHUNK
        potential = jnp.where(atom < atom_count[0], potential, 0.0)
        pre, sigma, out_w = hidden(features, w_in, w_out, lanes)
        lift = (sigma * (1.0 + pre * (1.0 - sigma)) * out_w).astype(BF16)
        grad = potential * dot(w_in[...], lift)
        for b in range(CHUNK // 128):
            rows = slice(c * CHUNK + b * 128, c * CHUNK + (b + 1) * 128)
            grads[rows, :] = jnp.transpose(grad[:, b * 128 : (b + 1) * 128]).astype(BF16)


VM = pl.BlockSpec(memory_space=pltpu.VMEM)
SM = pl.BlockSpec(memory_space=pltpu.SMEM)
PARAMS = pltpu.CompilerParams(vmem_limit_bytes=VMEM_LIMIT)


def spread(row_ids, slots, stencil_z, fractions, atom_count, features, w_in, w_out, basis):
    shape = jax.ShapeDtypeStruct
    return pl.pallas_call(
        spread_kernel,
        out_shape=(
            shape((DEVICES, ROWS), F32),
            shape((1, ROWS), F32),
            shape((ROWS, 128), F32),
            shape((1, ATOMS), F32),
            shape((1, ATOMS), jnp.int32),
        ),
        in_specs=[VM] * 4 + [SM] + [VM] * 4,
        out_specs=(VM,) * 5,
        scratch_shapes=[
            pltpu.VMEM((ROWS, 128), F32),
            pltpu.VMEM((2, 32, ATOMS), F32),
            pltpu.VMEM((16, ATOMS), F32),
            pltpu.VMEM((16, ATOMS), F32),
            pltpu.VMEM((ROWS, CHUNK), BF16),
            pltpu.VMEM((ROWS, CHUNK), BF16),
            pltpu.VMEM((GRID, CHUNK), BF16),
            pltpu.VMEM((GRID, CHUNK), BF16),
            pltpu.VMEM((GRID, ROWS), F32),
        ],
        compiler_params=PARAMS,
        name="spread",
    )(row_ids, slots, stencil_z, fractions, atom_count, features, w_in, w_out, basis)


def solve(rows, labels, tabs):
    return pl.pallas_call(
        solve_kernel,
        out_shape=jax.ShapeDtypeStruct((DEVICES, ROWS), F32),
        in_specs=[VM] * 3,
        out_specs=VM,
        scratch_shapes=[
            pltpu.VMEM((ROWS, GRID), F32),
            pltpu.VMEM((ROWS, GRID), F32),
            pltpu.VMEM((GRID, GRID), F32),
            pltpu.VMEM((ROWS, GRID), F32),
        ],
        compiler_params=PARAMS,
        name="solve",
    )(rows, labels, tabs)


def sample(
    returned, corner, charges, bins, stencil_z, fractions, atom_count, features, w_in, w_out, basis_t
):
    return pl.pallas_call(
        sample_kernel,
        out_shape=(
            jax.ShapeDtypeStruct((3, ATOMS), F32),
            jax.ShapeDtypeStruct((ATOMS, 128), BF16),
        ),
        in_specs=[VM] * 6 + [SM] + [VM] * 4,
        out_specs=(VM, VM),
        scratch_shapes=[
            pltpu.VMEM((3, 32, ATOMS), F32),
            pltpu.VMEM((24, ATOMS), F32),
            pltpu.VMEM((24, ATOMS), F32),
            pltpu.VMEM((GRID, ROWS), BF16),
            pltpu.VMEM((GRID, ROWS), BF16),
        ]
        + [pltpu.VMEM((ROWS, CHUNK), BF16)] * 6,
        compiler_params=PARAMS,
        name="sample",
    )(returned, corner, charges, bins, stencil_z, fractions, atom_count, features, w_in, w_out, basis_t)


def exchange(rows):
    return lax.all_to_all(rows, ("pen", "slab"), split_axis=0, concat_axis=0, tiled=True)


def local(features, fractions, row_ids, stencil_slots, stencil_z, atom_count, w_in, w_out):
    basis, basis_t, plane = tables()
    z_row = stencil_z.reshape(1, ATOMS)
    w_row = w_out.reshape(1, 128)
    sent, labels, bins, charges, corner = spread(
        row_ids, stencil_slots, z_row, fractions, atom_count, features, w_in, w_row, jnp.asarray(basis)
    )
    all_labels = lax.all_gather(labels, ("pen", "slab"), axis=0, tiled=True)
    replies = solve(exchange(sent), all_labels, jnp.asarray(plane))
    return sample(
        exchange(replies),
        corner,
        charges,
        bins,
        z_row,
        fractions,
        atom_count,
        features,
        w_in,
        w_row,
        jnp.asarray(basis_t),
    )


def solution(mesh):
    placed = (
        P(("pen", "slab"), None),
        P(None, ("pen", "slab")),
        P(("pen", "slab"), None),
        P(None, ("pen", "slab")),
        P(("pen", "slab")),
        P(("pen", "slab")),
        P(),
        P(),
    )
    return jax.shard_map(
        local,
        mesh=mesh,
        in_specs=placed,
        out_specs=(P(None, ("pen", "slab")), P(("pen", "slab"), None)),
        check_vma=False,
    )
```

time: 2190 us -> 163 us (0.07)
  local copies, waits for them, and re-layouts: 1080 us -> 7.1 us
  other arithmetic: 707 us -> 0 us
  starting transfers between devices: 276 us -> 15.7 us
  blocking collectives: 18.4 us -> 101 us
  waiting for transfers between devices: 66.2 us -> 0.01 us
  Pallas kernels: 0 us -> 36.7 us
  matrix products: 28.7 us -> 0 us
    gather x5 -> x0, local copies, waits for them, and re-layouts: 1040 us -> none  [the longest x2 1040 us: local(): samples = row_field[slot_index, z_index]]
    unnamed x7 -> x0, other arithmetic: 688 us -> none
    all_to_all x9 -> x1, starting transfers between devices: 276 us -> 15.7 us  [exchange(): lax.all_to_all(rows, ('pen', 'slab'), split_axis=0, concat_axis=0, tiled=...]
    all_gather x0 -> x1, blocking collectives: none -> 73.7 us  [local(): all_labels = lax.all_gather(labels, ('pen', 'slab'), axis=0, tiled=True)]
    all_to_all x9 -> x1, waiting for transfers between devices: 66.2 us -> 0.01 us  [exchange(): lax.all_to_all(rows, ('pen', 'slab'), split_axis=0, concat_axis=0, tiled=...]
    pallas_call x0 -> x3, Pallas kernels: none -> 36.7 us  [the longest x1 16.9 us: solve(): pl.pallas_call(solve_kernel, out_shape=jax.ShapeDtypeStruct((DEVICES, ROW...]
    dot_general x23 -> x0, matrix products: 28.7 us -> none  [the longest x20 25.8 us: contract(): lax.dot_general(left, right, (((left_dim,), (right_dim,)), ((), ())), pre...]
  transfers between devices with their start and end apart: 9 -> 1, of which waited for: 8 -> 0; matrix products, arithmetic and copies ran while one was open for 32% -> 1% of each run, Pallas kernels for 0% -> 0%
where the time goes in v1:
time: 163 us; the launch traced here: 162 us
  blocking collectives  101 us (62%)
  Pallas kernels  36.7 us (23%)
  starting transfers between devices  15.7 us (10%)
  local copies, waits for them, and re-layouts  7.1 us (4%)
    all_gather x1, blocking collectives, local(): all_labels = lax.all_gather(labels, ('pen', 'slab'), axis=0, tiled=True)  73.7 us
    all_to_all x1, blocking collectives, exchange(): lax.all_to_all(rows, ('pen', 'slab'), split_axis=0, concat_axis=0, tiled=...  27.8 us
    pallas_call x1, Pallas kernels, solve(): pl.pallas_call(solve_kernel, out_shape=jax.ShapeDtypeStruct((DEVICES, ROW...  16.9 us
    all_to_all x1, starting transfers between devices, exchange(): lax.all_to_all(rows, ('pen', 'slab'), split_axis=0, concat_axis=0, tiled=...  15.7 us
    pallas_call x1, Pallas kernels, sample(): pl.pallas_call(sample_kernel, out_shape=(jax.ShapeDtypeStruct((3, ATOMS),...  12.5 us
    pallas_call x1, Pallas kernels, spread(): pl.pallas_call(spread_kernel, out_shape=(shape((DEVICES, ROWS), F32), sha...  7.36 us
    all_to_all x2, local copies, waits for them, and re-layouts, exchange(): lax.all_to_all(rows, ('pen', 'slab'), split_axis=0, concat_axis=0, tiled=...  3.94 us
  transfers between devices with their start and end apart: 1, of which 0 were waited for; matrix products, arithmetic and copies ran while one was open for 1% of the time, Pallas kernels for 0%

profile of v1, /device:TPU:1, one launch (start us, length us, event | category | flops | bytes accessed | tf_op | source)
XLA Modules:
  0.0 162.2 jit_solution(13574440813911049363)
XLA Ops:
  1.3 7.4 %spread.1 = (f32[256,512]{1,0:T(8,128)}, f32[1,512]{1,0:T(1,128)}, f32[512,128]{1,0:T(8,128)}, f32[1,2048]{1,0:T(1,128)}, s32[1,2048]{1,0:T(1,128)}) custom-call(s32[1,512]{1,0:T(1,128)} %row_ids.1, s32[16,2048]{1,0:T(8,128)} %slots.1, s32[1,2048]{1,0:T(1,128)} %bitcast.19, f32[3,2048]{1,0:T(4,128)} %fractions.3, s32[1]{0:T(128)S(6)} %copy.24.atom_count, ...), custom_call_target="tpu_custom_call" | custom-call | tf_op jit(solution)/shard_map/spread/pallas_call | solution.py:421
  8.6 2.4 %copy.13 = f32[256,1,512]{2,1,0:T(1,128)} copy(f32[256,1,512]{2,0,1:T(8,128)} %bitcast.18) | data formatting | bytes 1048576 | tf_op jit(solution)/shard_map/all_to_all | solution.py:490
  11.0 15.7 %all-to-all-start = ((f32[256,1,512]{2,1,0:T(1,128)}), f32[256,1,512]{2,1,0:T(1,128)S(1)}, u32[]{:S(2)}, u32[]{:S(2)}) async-start(f32[256,1,512]{2,1,0:T(1,128)} %copy.13), calls=%async_computation | async-start | bytes 1048576 | tf_op jit(solution)/shard_map/all_to_all | solution.py:490
  26.7 0.0 copy-start
  26.7 0.7 copy-done
  27.4 73.7 %all-gather = f32[256,1,512]{2,1,0:T(1,128)S(1)} all-gather(f32[1,1,512]{2,1,0:T(1,128)S(1)} %bitcast.21), channel_id=1, replica_groups=mesh['pen'=32,'slab'=8] {'pen','slab'}, dimensions={0}, use_global_device_ids=true | all-gather | bytes 526336 | tf_op jit(solution)/shard_map/all_gather | solution.py:500
  101.1 0.8 copy.22
  101.9 0.0 all-to-all-done
  101.9 0.8 copy.23
  102.7 16.9 %solve.1 = f32[256,512]{1,0:T(8,128)} custom-call(f32[256,512]{1,0:T(8,128)} %bitcast.16, f32[256,512]{1,0:T(8,128)} %bitcast.15, bf16[6,256,256]{2,1,0:T(8,128)(2,1)} %constant.7.clone.tabs), custom_call_target="tpu_custom_call" | custom-call | tf_op jit(solution)/shard_map/solve/pallas_call | solution.py:449
  119.6 1.6 copy.14
  121.2 27.8 %all_to_all.22 = f32[256,1,512]{2,1,0:T(1,128)S(1)} all-to-all(f32[256,1,512]{2,1,0:T(1,128)S(1)} %copy.14), channel_id=1, replica_groups=mesh['pen'=32,'slab'=8] {'pen','slab'}, dimensions={0} | all-to-all | bytes 1048576 | tf_op jit(solution)/shard_map/all_to_all | solution.py:490
  148.9 0.8 copy.21
  149.7 12.5 %sample.1 = (f32[3,2048]{1,0:T(4,128)}, bf16[2048,128]{1,0:T(8,128)(2,1)}) custom-call(f32[256,512]{1,0:T(8,128)} %bitcast.14, s32[1,2048]{1,0:T(1,128)} %get-tuple-element.9.corner, f32[1,2048]{1,0:T(1,128)} %get-tuple-element.10.charges, f32[512,128]{1,0:T(8,128)} %get-tuple-element.11.bins_cols, s32[1,2048]{1,0:T(1,128)} %bitcast.20, ...), custom_call_target="tpu_custom_call" | custom-call | tf_op jit(solution)/shard_map/sample/pallas_call | solution.py:468
Async XLA Ops:
  11.0 90.9 %all-to-all-start = ((f32[256,1,512]{2,1,0:T(1,128)}), f32[256,1,512]{2,1,0:T(1,128)S(1)}, u32[]{:S(2)}, u32[]{:S(2)}) async-start(f32[256,1,512]{2,1,0:T(1,128)} %copy.13), calls=%async_computation | async-start | bytes 1048576 | tf_op jit(solution)/shard_map/all_to_all | solution.py:490
  26.7 0.7 copy-start

commit v2 on v1

v2 whole, which is shorter than its diff:
```python
import functools
import math

import jax
import jax.numpy as jnp
import ml_dtypes
import numpy as np
from jax import lax
from jax.experimental import pallas as pl
from jax.experimental.pallas import tpu as pltpu
from jax.sharding import PartitionSpec as P

GRID = 256
COUPLE = 8.0
SMOOTH = 1.0
ROWS = 512
ATOMS = 2048
DEVICES = 256
CHUNK = 512
VMEM_LIMIT = 56 * 1024 * 1024
F32 = jnp.float32
BF16 = jnp.bfloat16

NN = (((1,), (0,)), ((), ()))
NT = (((1,), (1,)), ((), ()))


def dot(left, right, dims=NN):
    return lax.dot_general(left, right, dims, preferred_element_type=F32)


def split(value):
    high = value.astype(BF16)
    low = (value - high.astype(F32)).astype(BF16)
    return (high, low)


def dot3(left, right, dims=NN):
    return (
        dot(left[0], right[0], dims)
        + dot(left[0], right[1], dims)
        + dot(left[1], right[0], dims)
    )


def fourier_basis():
    cell = np.arange(GRID)
    wave = np.arange(GRID)
    wave = np.where(wave <= GRID // 2, wave, wave - GRID // 2)
    angle = 2.0 * np.pi * ((wave[:, None] * cell[None, :]) % GRID) / GRID
    basis = np.where(np.arange(GRID)[:, None] <= GRID // 2, np.cos(angle), np.sin(angle))
    scale = np.where((np.arange(GRID) == 0) | (np.arange(GRID) == GRID // 2), 1.0, 2.0)
    return basis * np.sqrt(scale / GRID)[:, None]


def split_table(table):
    table = table.astype(np.float32)
    high = table.astype(ml_dtypes.bfloat16)
    low = (table - high.astype(np.float32)).astype(ml_dtypes.bfloat16)
    return [high, low]


def tables():
    basis = fourier_basis()
    place = np.arange(GRID)
    along_x = basis[:, (place % 8) * 32 + place // 8]
    along_y = basis[:, (place % 32) * 8 + place // 32]
    plane = np.stack(split_table(along_x) + split_table(along_x.T) + split_table(along_y))
    return (np.stack(split_table(basis)), np.stack(split_table(basis.T)), plane)


def spline_values(u):
    rest = 1.0 - u
    square = u * u
    cube = square * u
    return (
        rest * rest * rest / 6.0,
        (3.0 * cube - 6.0 * square + 4.0) / 6.0,
        (-3.0 * cube + 3.0 * square + 3.0 * u + 1.0) / 6.0,
        cube / 6.0,
    )


def spline_slopes(u):
    rest = 1.0 - u
    square = u * u
    return (
        -rest * rest / 2.0,
        (3.0 * square - 4.0 * u) / 2.0,
        (-3.0 * square + 2.0 * u + 1.0) / 2.0,
        square / 2.0,
    )


def pick(step, values):
    out = jnp.where(step == 3, values[3], 0.0)
    for k in (2, 1, 0):
        out = jnp.where(step == k, values[k], out)
    return out


def row_to_columns(row):
    return jnp.transpose(jnp.broadcast_to(row, (128, 128)))


def bin_labels(row_ids, ids_cols, bins_cols):
    ids = row_ids[...]
    used = ids >= 0
    x = ids >> 8
    y = ids & 255
    group = jnp.where(used, (x & 31) * 8 + (y & 7), -1)
    label = ((x >> 5) * 32 + (y >> 3)).astype(F32)
    group_f = group.astype(F32)
    place = lax.broadcasted_iota(jnp.int32, (128, ROWS), 1)
    row = lax.broadcasted_iota(jnp.int32, (128, ROWS), 0)
    rank = jnp.zeros((1, ROWS), F32)
    for c in range(ROWS // 128):
        lanes = slice(c * 128, (c + 1) * 128)
        ids_cols[lanes, :] = row_to_columns(ids[:, lanes].astype(F32))
        column = row_to_columns(group_f[:, lanes])
        column = jnp.concatenate([column] * (ROWS // 128), axis=1)
        same = (column == group_f) & (row + c * 128 < place)
        rank += jnp.sum(jnp.where(same, 1.0, 0.0), axis=0, keepdims=True)
    target = jnp.where(used, rank.astype(jnp.int32) * 256 + group, -1)
    for c in range(ROWS // 128):
        hit = target == row + c * 128
        value = jnp.sum(jnp.where(hit, label + 1.0, 0.0), axis=1, keepdims=True) - 1.0
        bins_cols[c * 128 : (c + 1) * 128, :] = jnp.broadcast_to(value, (128, 128))


def corners(slots, ids_cols, corner):
    row = lax.broadcasted_iota(jnp.int32, (ROWS, 128), 0)
    for c in range(ATOMS // 128):
        lanes = slice(c * 128, (c + 1) * 128)
        hit = slots[0:1, lanes] == row
        value = jnp.sum(jnp.where(hit, ids_cols[...], 0.0), axis=0, keepdims=True)
        corner[0:1, lanes] = value.astype(jnp.int32)


def class_weights(corner, fractions, tab_x, tab_y, slopes):
    x0 = corner[0:1, :] >> 8
    y0 = corner[0:1, :] & 255
    value_x = spline_values(fractions[0:1, :])
    value_y = spline_values(fractions[1:2, :])
    step_y = (lax.broadcasted_iota(jnp.int32, (8, ATOMS), 0) - y0) & 7
    tab_y[0:8, :] = pick(step_y, value_y)
    tab_y[8:16, :] = ((((y0 + step_y) >> 3) & 31)).astype(F32)
    if slopes:
        slope_x = spline_slopes(fractions[0:1, :])
        slope_y = spline_slopes(fractions[1:2, :])
        tab_y[16:24, :] = pick(step_y, slope_y)
    for b in range(4):
        rows = slice(b * 8, (b + 1) * 8)
        step_x = (lax.broadcasted_iota(jnp.int32, (8, ATOMS), 0) + b * 8 - x0) & 31
        tab_x[0, rows, :] = pick(step_x, value_x)
        tab_x[1, rows, :] = ((((x0 + step_x) >> 5) & 7) * 32).astype(F32)
        if slopes:
            tab_x[2, rows, :] = pick(step_x, slope_x)


def class_weights_z(stencil_z, fractions, tab_z, slopes):
    z0 = stencil_z[0:1, :]
    step_z = (lax.broadcasted_iota(jnp.int32, (8, ATOMS), 0) - z0) & 7
    tab_z[0:8, :] = pick(step_z, spline_values(fractions[2:3, :]))
    tab_z[8:16, :] = ((((z0 + step_z) >> 3) & 31)).astype(F32)
    if slopes:
        tab_z[16:24, :] = pick(step_z, spline_slopes(fractions[2:3, :]))


def row_weights(tab_x, tab_y, bins_cols, lanes, outs, first, last):
    def twice(part):
        return jnp.concatenate([part, part], axis=0)

    wy = twice(tab_y[0:8, lanes])
    ky = twice(tab_y[8:16, lanes])
    sy = twice(tab_y[16:24, lanes])
    width = wy.shape[1]

    def pair(index, i):
        rows = [tab_x[index, pl.ds(2 * i + k, 1), lanes] for k in range(2)]
        return jnp.concatenate([jnp.broadcast_to(row, (8, width)) for row in rows], axis=0)

    @pl.loop(0, 16)
    def _(i):
        wx = pair(0, i)
        key = pair(1, i) + ky
        values = [wx * wy, pair(2, i) * wy, wx * sy][first:last]
        for rank in range(2):
            rows = pl.ds(pl.multiple_of(rank * 256 + i * 16, 16), 16)
            label = bins_cols[rows, :]
            label = jnp.concatenate([label] * (width // 128), axis=1)
            hit = key == label
            for k, value in enumerate(values):
                high, low = split(jnp.where(hit, value, 0.0))
                outs[2 * k][rows, :] = high
                outs[2 * k + 1][rows, :] = low


def hidden(features, w_in, w_out, lanes):
    w_in_t = jnp.transpose(w_in[...].astype(F32)).astype(BF16)
    pre = dot(w_in_t, features[lanes, :], NT)
    sigma = jax.nn.sigmoid(pre)
    out_w = row_to_columns(w_out[...])
    out_w = jnp.concatenate([out_w] * (pre.shape[1] // 128), axis=1)
    return (pre, sigma, out_w)


MESH = pl.DeviceIdType.MESH
DZ = (4, 1, 7, 2, 6, 3, 5, 0)


def here():
    pen = lax.axis_index("pen")
    slab = lax.axis_index("slab")
    return (pen // 4, lax.rem(pen, 4), slab // 2, lax.rem(slab, 2))


def place_of(z, y, x, core):
    return ((core * 4 + x) * 4 + y) * 8 + z


def target_of(z, y, x, core):
    return (z * 4 + y, x * 2 + core)


def for_all_others(visit):
    z, y, x, core = here()

    @pl.loop(0, 32)
    def _(k):
        other_y = lax.rem(y + lax.rem(k, 4), 4)
        other_x = lax.rem(x + lax.rem(k // 4, 4), 4)
        other_core = lax.rem(core + k // 16, 2)
        for dz in DZ:
            there = (lax.rem(z + dz, 8), other_y, other_x, other_core)
            if dz == 0:
                pl.when(k > 0)(functools.partial(visit, there))
            else:
                visit(there)


def enter():
    barrier = pltpu.get_barrier_semaphore()

    def greet(there):
        pl.semaphore_signal(barrier, inc=1, device_id=target_of(*there), device_id_type=MESH)

    for_all_others(greet)
    return barrier


def send_rows(rows, landed, spare, send_sem, recv_sem):
    me = place_of(*here())
    pltpu.make_async_copy(rows.at[me], landed.at[me], recv_sem).start()
    pltpu.make_async_copy(rows.at[me], spare, send_sem).start()

    def send(there):
        pltpu.make_async_remote_copy(
            src_ref=rows.at[place_of(*there)],
            dst_ref=landed.at[me],
            send_sem=send_sem,
            recv_sem=recv_sem,
            device_id=target_of(*there),
            device_id_type=MESH,
        ).start()

    for_all_others(send)


def await_rows(rows, landed, sem):
    pltpu.make_async_copy(rows, landed, sem).wait()


def label_copies(stage, all_labels, send_sems, recv_sems):
    z, y, x, core = here()
    if stage == 0:
        part = all_labels.at[core, x, y, z]
        peers = [(lax.rem(z + k, 8), y, x, core) for k in range(1, 8)]
        first = 0
    elif stage == 1:
        part = all_labels.at[core, x, y]
        peers = [(z, lax.rem(y + k, 4), x, core) for k in range(1, 4)]
        first = 7
    elif stage == 2:
        part = all_labels.at[core, x]
        peers = [(z, y, lax.rem(x + k, 4), core) for k in range(1, 4)]
        first = 10
    else:
        part = all_labels.at[core]
        peers = [(z, y, x, 1 - core)]
        first = 13
    return [
        pltpu.make_async_remote_copy(
            src_ref=part,
            dst_ref=part,
            send_sem=send_sems.at[first + k],
            recv_sem=recv_sems.at[first + k],
            device_id=target_of(*peer),
            device_id_type=MESH,
        )
        for k, peer in enumerate(peers)
    ]


def step_kernel(
    row_ids,
    slots,
    stencil_z,
    fractions,
    atom_count,
    features,
    w_in,
    w_out,
    basis,
    basis_t,
    tabs,
    forces,
    grads,
    ids_cols,
    bins_cols,
    own_labels,
    all_labels,
    charges,
    corner,
    tab_x,
    tab_y,
    tab_z,
    z_high,
    z_low,
    mesh_rows,
    sent,
    arrived,
    rows_t,
    labels_t,
    onehot_y,
    plane,
    replies_t,
    replies,
    returned,
    spare,
    lifts,
    kernel,
    field_high,
    field_low,
    weights,
    label_send,
    label_recv,
    sem_own,
    send_one,
    recv_one,
    send_two,
    recv_two,
):
    barrier = enter()
    z, y, x, core = here()
    bin_labels(row_ids, ids_cols, bins_cols)
    for c in range(ROWS // 128):
        part = jnp.transpose(bins_cols[c * 128 : (c + 1) * 128, :])
        own_labels[0:1, c * 128 : (c + 1) * 128] = part[0:1, :]
    pl.semaphore_wait(barrier, DEVICES - 1)
    mine = pltpu.make_async_copy(own_labels.at[0], all_labels.at[core, x, y, z], sem_own)
    mine.start()
    mine.wait()

    def labels_on(stage):
        if stage > 0:
            for copy in label_copies(stage - 1, all_labels, label_send, label_recv):
                copy.wait()
        if stage < 4:
            for copy in label_copies(stage, all_labels, label_send, label_recv):
                copy.start()

    labels_on(0)
    corners(slots, ids_cols, corner)
    class_weights(corner, fractions, tab_x, tab_y, True)
    class_weights_z(stencil_z, fractions, tab_z, True)
    labels_on(1)
    for c in range(ATOMS // CHUNK):
        lanes = slice(c * CHUNK, (c + 1) * CHUNK)
        pre, sigma, out_w = hidden(features, w_in, w_out, lanes)
        charge = jnp.sum(pre * sigma * out_w, axis=0, keepdims=True)
        atom = lax.broadcasted_iota(jnp.int32, (1, CHUNK), 1) + c * CHUNK
        charges[0:1, lanes] = jnp.where(atom < atom_count[0], charge, 0.0)
        lifts[:, lanes] = (sigma * (1.0 + pre * (1.0 - sigma)) * out_w).astype(BF16)
    labels_on(2)
    for c in range(ATOMS // CHUNK):
        lanes = slice(c * CHUNK, (c + 1) * CHUNK)
        row_weights(tab_x, tab_y, bins_cols, lanes, [weights.at[k, c] for k in range(2)], 0, 1)
        key = tab_z[8:16, lanes]
        amount = tab_z[0:8, lanes] * charges[0:1, lanes]
        amount_high = amount.astype(BF16).astype(F32)
        amount_low = amount - amount_high
        for h in range(0, 32, 2):
            rows = slice(h * 8, h * 8 + 16)
            hits = (key == float(h), key == float(h + 1))
            z_high[rows, :] = jnp.concatenate(
                [jnp.where(hit, amount_high, 0.0) for hit in hits], axis=0
            ).astype(BF16)
            z_low[rows, :] = jnp.concatenate(
                [jnp.where(hit, amount_low, 0.0) for hit in hits], axis=0
            ).astype(BF16)
        total = dot3((z_high[...], z_low[...]), (weights[0, c], weights[1, c]), NT)
        if c == 0:
            mesh_rows[...] = total
        else:
            mesh_rows[...] += total
        if c == 1:
            labels_on(3)
    sent[...] = dot3((basis[0], basis[1]), split(mesh_rows[...]))
    send_rows(sent, arrived, spare, send_one, recv_one)
    labels_on(4)

    blocks = DEVICES // 2
    for b in range(2):
        for c in range(ROWS // 128):
            part = all_labels[b, :, :, :, c * 128 : (c + 1) * 128].reshape(128, 128)
            dst = (slice(c * 128, (c + 1) * 128), slice(b * 128, (b + 1) * 128))
            labels_t[dst] = jnp.transpose(part)
    cell_y = lax.broadcasted_iota(jnp.int32, (32, GRID), 0).astype(F32)

    @pl.loop(0, 32)
    def _(xb):
        for rank in range(2):
            label = labels_t[pl.ds(pl.multiple_of(rank * 256 + xb * 8, 8), 8), :]
            label_y = label - 32.0 * jnp.floor(label * (1.0 / 32.0))
            for yb in range(8):
                hit = jnp.broadcast_to(label_y[yb : yb + 1], (32, GRID)) == cell_y
                onehot_y[xb * 8 + yb, :, rank * GRID : (rank + 1) * GRID] = jnp.where(
                    hit, 1.0, 0.0
                ).astype(BF16)

    for c in range(ATOMS // CHUNK):
        lanes = slice(c * CHUNK, (c + 1) * CHUNK)
        row_weights(tab_x, tab_y, bins_cols, lanes, [weights.at[k, c] for k in range(2, 6)], 1, 3)
    coulomb(kernel, place_of(z, y, x, core))
    await_rows(sent, arrived, recv_one)

    for b in range(2):
        for c in range(ROWS // 128):
            src = (slice(b * 128, (b + 1) * 128), slice(c * 128, (c + 1) * 128))
            dst = (slice(c * 128, (c + 1) * 128), slice(b * 128, (b + 1) * 128))
            rows_t[dst] = jnp.transpose(arrived[src])
    solve_plane(rows_t, labels_t, onehot_y, tabs, kernel, plane, replies_t)
    for b in range(2):
        for c in range(ROWS // 128):
            src = (slice(c * 128, (c + 1) * 128), slice(b * 128, (b + 1) * 128))
            dst = (slice(b * 128, (b + 1) * 128), slice(c * 128, (c + 1) * 128))
            replies[dst] = jnp.transpose(replies_t[src])
    await_rows(sent, arrived, send_one)
    send_rows(replies, returned, spare, send_two, recv_two)
    await_rows(replies, returned, recv_two)

    field_high[...], field_low[...] = split(
        dot3((basis_t[0], basis_t[1]), split(returned[...]))
    )
    for c in range(ATOMS // CHUNK):
        lanes = slice(c * CHUNK, (c + 1) * CHUNK)
        key = tab_z[8:16, lanes]
        sums = []
        for k in range(3):
            total = dot3(
                (field_high[...], field_low[...]), (weights[2 * k, c], weights[2 * k + 1, c])
            )
            chosen = jnp.zeros((8, CHUNK), F32)
            for h in range(32):
                chosen = jnp.where(key == float(h), total[h * 8 : (h + 1) * 8], chosen)
            sums.append(chosen)
        wz = tab_z[0:8, lanes]
        potential = jnp.sum(wz * sums[0], axis=0, keepdims=True)
        charge = -charges[0:1, lanes]
        forces[0:1, lanes] = charge * jnp.sum(wz * sums[1], axis=0, keepdims=True)
        forces[1:2, lanes] = charge * jnp.sum(wz * sums[2], axis=0, keepdims=True)
        forces[2:3, lanes] = charge * jnp.sum(tab_z[16:24, lanes] * sums[0], axis=0, keepdims=True)
        atom = lax.broadcasted_iota(jnp.int32, (1, CHUNK), 1) + c * CHUNK
        potential = jnp.where(atom < atom_count[0], potential, 0.0)
        grad = potential * dot(w_in[...], lifts[:, lanes])
        for b in range(CHUNK // 128):
            rows = slice(c * CHUNK + b * 128, c * CHUNK + (b + 1) * 128)
            grads[rows, :] = jnp.transpose(grad[:, b * 128 : (b + 1) * 128]).astype(BF16)
    await_rows(replies, returned, send_two)


def coulomb(kernel, wave_index):
    half = GRID // 2

    def wave(index):
        return jnp.where(index <= half, index, index - half)

    wave_x = wave(lax.broadcasted_iota(jnp.int32, (GRID, GRID), 0))
    wave_y = wave(lax.broadcasted_iota(jnp.int32, (GRID, GRID), 1))
    wave_z = wave(wave_index)
    squared = (wave_x * wave_x + wave_y * wave_y + wave_z * wave_z).astype(F32)
    damped = jnp.exp(-((SMOOTH * math.pi / GRID) ** 2) * squared)
    values = COUPLE * damped * (GRID * GRID) / (4.0 * math.pi * math.pi * jnp.maximum(squared, 1.0))
    keep = (squared > 0) & (wave_x != half) & (wave_y != half) & (wave_z != half)
    kernel[...] = jnp.where(keep, values, 0.0)


def solve_plane(rows_t, labels_t, onehot_y, tabs, kernel, plane, replies_t):
    lane_class = lax.broadcasted_iota(jnp.int32, (8, GRID), 0).astype(F32)

    @pl.loop(0, 32)
    def _(xb):
        groups = []
        for rank in range(2):
            at = pl.ds(pl.multiple_of(rank * 256 + xb * 8, 8), 8)
            value = rows_t[at, :]
            value_high = value.astype(BF16).astype(F32)
            label_x = jnp.floor(labels_t[at, :] * (1.0 / 32.0))
            groups.append((value_high, value - value_high, label_x))
        pieces = []
        for yb in range(8):
            left = []
            for value_high, value_low, label_x in groups:
                hit = jnp.broadcast_to(label_x[yb : yb + 1], (8, GRID)) == lane_class
                both = [
                    jnp.where(hit, jnp.broadcast_to(part[yb : yb + 1], (8, GRID)), 0.0)
                    for part in (value_high, value_low)
                ]
                left.append(jnp.concatenate(both, axis=0).astype(BF16))
            piece = dot(jnp.concatenate(left, axis=1), onehot_y[xb * 8 + yb], NT)
            pieces.append(piece[0:8] + piece[8:16])
        plane[pl.ds(pl.multiple_of(xb * 8, 8), 8), :] = jnp.concatenate(pieces, axis=1)

    along_x, back_x, along_y = [(tabs[2 * k], tabs[2 * k + 1]) for k in range(3)]
    spectrum = dot3(along_x, split(plane[...]))
    spectrum = dot3(split(spectrum), along_y, NT) * kernel[...]
    field = dot3(back_x, split(spectrum))
    plane[...] = dot3(split(field), along_y)

    upper = lax.broadcasted_iota(jnp.int32, (8, 128), 0) >= 4
    offset = (lax.broadcasted_iota(jnp.int32, (8, 128), 0) & 3) * 32

    @pl.loop(0, 32)
    def _(xb):
        sources = []
        field_rows = plane[pl.ds(pl.multiple_of(xb * 8, 8), 8), :]
        for h in range(8):
            row = jnp.broadcast_to(field_rows[h : h + 1], (8, GRID))
            sources.append(jnp.where(upper, row[:, 128:], row[:, :128]))
        for rank in range(2):
            at = pl.ds(pl.multiple_of(rank * 256 + xb * 8, 8), 8)
            for b in range(2):
                label = labels_t[at, b * 128 : (b + 1) * 128].astype(jnp.int32)
                label_x = label >> 5
                index = (label & 31) + offset
                value = jnp.zeros((8, 128), F32)
                for h in range(8):
                    taken = jnp.take_along_axis(
                        sources[h], index, axis=1, mode="promise_in_bounds"
                    )
                    value = jnp.where(label_x == h, taken, value)
                replies_t[at, b * 128 : (b + 1) * 128] = value


VM = pl.BlockSpec(memory_space=pltpu.VMEM)
SM = pl.BlockSpec(memory_space=pltpu.SMEM)


def local(features, fractions, row_ids, stencil_slots, stencil_z, atom_count, w_in, w_out):
    basis, basis_t, plane = [jnp.asarray(table) for table in tables()]
    vmem = pltpu.VMEM
    chunks = ATOMS // CHUNK
    return pl.pallas_call(
        step_kernel,
        out_shape=(
            jax.ShapeDtypeStruct((3, ATOMS), F32),
            jax.ShapeDtypeStruct((ATOMS, 128), BF16),
        ),
        in_specs=[VM] * 4 + [SM] + [VM] * 6,
        out_specs=(VM, VM),
        scratch_shapes=[
            vmem((ROWS, 128), F32),
            vmem((ROWS, 128), F32),
            vmem((8, ROWS), F32),
            vmem((2, 4, 4, 8, ROWS), F32),
            vmem((1, ATOMS), F32),
            vmem((1, ATOMS), jnp.int32),
            vmem((3, 32, ATOMS), F32),
            vmem((24, ATOMS), F32),
            vmem((24, ATOMS), F32),
            vmem((GRID, CHUNK), BF16),
            vmem((GRID, CHUNK), BF16),
            vmem((GRID, ROWS), F32),
            vmem((DEVICES, ROWS), F32),
            vmem((DEVICES, ROWS), F32),
            vmem((ROWS, GRID), F32),
            vmem((ROWS, GRID), F32),
            vmem((GRID, 32, 2 * GRID), BF16),
            vmem((GRID, GRID), F32),
            vmem((ROWS, GRID), F32),
            vmem((DEVICES, ROWS), F32),
            vmem((DEVICES, ROWS), F32),
            vmem((ROWS,), F32),
            vmem((128, ATOMS), BF16),
            vmem((GRID, GRID), F32),
            vmem((GRID, ROWS), BF16),
            vmem((GRID, ROWS), BF16),
            vmem((6, chunks, ROWS, CHUNK), BF16),
            pltpu.SemaphoreType.DMA((14,)),
            pltpu.SemaphoreType.DMA((14,)),
        ]
        + [pltpu.SemaphoreType.DMA] * 5,
        compiler_params=pltpu.CompilerParams(
            vmem_limit_bytes=VMEM_LIMIT, collective_id=0, has_side_effects=True
        ),
        name="step",
    )(
        row_ids,
        stencil_slots,
        stencil_z.reshape(1, ATOMS),
        fractions,
        atom_count,
        features,
        w_in,
        w_out.reshape(1, 128),
        basis,
        basis_t,
        plane,
    )


def solution(mesh):
    placed = (
        P(("pen", "slab"), None),
        P(None, ("pen", "slab")),
        P(("pen", "slab"), None),
        P(None, ("pen", "slab")),
        P(("pen", "slab")),
        P(("pen", "slab")),
        P(),
        P(),
    )
    return jax.shard_map(
        local,
        mesh=mesh,
        in_specs=placed,
        out_specs=(P(None, ("pen", "slab")), P(("pen", "slab"), None)),
        check_vma=False,
    )
```

time: 163 us -> 86.1 us (0.53)
  blocking collectives: 101 us -> 0 us
  Pallas kernels: 36.7 us -> 81.4 us
  starting transfers between devices: 15.7 us -> 0 us
  local copies, waits for them, and re-layouts: 7.1 us -> 3.25 us
    all_gather x1 -> x0, blocking collectives: 73.7 us -> none  [local(): all_labels = lax.all_gather(labels, ('pen', 'slab'), axis=0, tiled=True)]
    pallas_call x3 -> x1, Pallas kernels: 36.7 us -> 81.4 us  [local(): pl.pallas_call(step_kernel, out_shape=(jax.ShapeDtypeStruct((3, ATOMS), F...]
    all_to_all x1 -> x0, blocking collectives: 27.8 us -> none  [exchange(): lax.all_to_all(rows, ('pen', 'slab'), split_axis=0, concat_axis=0, tiled=...]
    all_to_all x1 -> x0, starting transfers between devices: 15.7 us -> none  [exchange(): lax.all_to_all(rows, ('pen', 'slab'), split_axis=0, concat_axis=0, tiled=...]
    all_to_all x2 -> x0, local copies, waits for them, and re-layouts: 3.94 us -> none  [exchange(): lax.all_to_all(rows, ('pen', 'slab'), split_axis=0, concat_axis=0, tiled=...]
  transfers between devices with their start and end apart: 1 -> 0, of which waited for: 0 -> 0; matrix products, arithmetic and copies ran while one was open for 1% -> 0% of each run, Pallas kernels for 0% -> 0%
where the time goes in v2:
time: 86.1 us; the launch traced here: 85.9 us
  Pallas kernels  81.4 us (95%)
  local copies, waits for them, and re-layouts  3.25 us (4%)
  between operations  1.29 us (1%)
    pallas_call x1, Pallas kernels, local(): pl.pallas_call(step_kernel, out_shape=(jax.ShapeDtypeStruct((3, ATOMS), F...  81.4 us
    unnamed x2, local copies, waits for them, and re-layouts  3.25 us

profile of v2, /device:TPU:1, one launch (start us, length us, event | category | flops | bytes accessed | tf_op | source)
XLA Modules:
  0.0 85.9 jit_solution(16387046235287787198)
XLA Ops:
  1.3 81.4 %step.1 = (f32[3,2048]{1,0:T(4,128)}, bf16[2048,128]{1,0:T(8,128)(2,1)}) custom-call(s32[1,512]{1,0:T(1,128)} %row_ids.1, s32[16,2048]{1,0:T(8,128)} %slots.1, s32[1,2048]{1,0:T(1,128)} %bitcast.2, f32[3,2048]{1,0:T(4,128)} %fractions.1, s32[1]{0:T(128)S(6)} %copy.15.atom_count, bf16[2048,128]{1,0:T(8,128)(2,1)} %features.1, bf16[128,128]{1,0:T(8,128)(2,1)} %w_in.1, ...), custom_call_target="tpu_custom_call" | custom-call | tf_op jit(solution)/shard_map/step/pallas_call | solution.py:564
  82.6 1.4 %copy.16 = f32[3,2048]{1,0:T(4,128)} copy(f32[3,2048]{1,0:T(4,128)} %get-tuple-element.4) | data formatting | bytes 49152
  84.0 1.9 %copy.17 = bf16[2048,128]{1,0:T(8,128)(2,1)} copy(bf16[2048,128]{1,0:T(8,128)(2,1)} %get-tuple-element.5) | data formatting | bytes 1048576

commit v3 on v2

--- a/solution.py
+++ b/solution.py
@@ -110,16 +110,16 @@
     y = ids & 255
     group = jnp.where(used, (x & 31) * 8 + (y & 7), -1)
     label = ((x >> 5) * 32 + (y >> 3)).astype(F32)
-    group_f = group.astype(F32)
     place = lax.broadcasted_iota(jnp.int32, (128, ROWS), 1)
     row = lax.broadcasted_iota(jnp.int32, (128, ROWS), 0)
     rank = jnp.zeros((1, ROWS), F32)
     for c in range(ROWS // 128):
         lanes = slice(c * 128, (c + 1) * 128)
-        ids_cols[lanes, :] = row_to_columns(ids[:, lanes].astype(F32))
-        column = row_to_columns(group_f[:, lanes])
+        column = row_to_columns(ids[:, lanes])
+        ids_cols[lanes, :] = column.astype(F32)
+        column = (column >> 8 & 31) * 8 + (column & 7)
         column = jnp.concatenate([column] * (ROWS // 128), axis=1)
-        same = (column == group_f) & (row + c * 128 < place)
+        same = (column == group) & (row + c * 128 < place)
         rank += jnp.sum(jnp.where(same, 1.0, 0.0), axis=0, keepdims=True)
     target = jnp.where(used, rank.astype(jnp.int32) * 256 + group, -1)
     for c in range(ROWS // 128):
@@ -223,72 +223,60 @@
     return (z * 4 + y, x * 2 + core)
 
 
-def for_all_others(visit):
+def for_others(half, visit):
     z, y, x, core = here()
-
-    @pl.loop(0, 32)
+    other_core = lax.rem(core + half, 2)
+
+    @pl.loop(0, 16)
     def _(k):
         other_y = lax.rem(y + lax.rem(k, 4), 4)
-        other_x = lax.rem(x + lax.rem(k // 4, 4), 4)
-        other_core = lax.rem(core + k // 16, 2)
+        other_x = lax.rem(x + k // 4, 4)
         for dz in DZ:
             there = (lax.rem(z + dz, 8), other_y, other_x, other_core)
-            if dz == 0:
+            if dz == 0 and half == 0:
                 pl.when(k > 0)(functools.partial(visit, there))
             else:
                 visit(there)
 
 
-def enter():
-    barrier = pltpu.get_barrier_semaphore()
-
-    def greet(there):
-        pl.semaphore_signal(barrier, inc=1, device_id=target_of(*there), device_id_type=MESH)
-
-    for_all_others(greet)
-    return barrier
-
-
-def send_rows(rows, landed, spare, send_sem, recv_sem):
-    me = place_of(*here())
-    pltpu.make_async_copy(rows.at[me], landed.at[me], recv_sem).start()
-    pltpu.make_async_copy(rows.at[me], spare, send_sem).start()
-
+def lines():
+    z, y, x, core = here()
+    return (
+        [(lax.rem(z + k, 8), y, x, core) for k in range(1, 8)],
+        [(z, lax.rem(y + k, 4), x, core) for k in range(1, 4)],
+        [(z, y, lax.rem(x + k, 4), core) for k in range(1, 4)],
+        [(z, y, x, 1 - core)],
+    )
+
+
+def send_half(half, row_of, landed, send_sem, recv_sem):
     def send(there):
         pltpu.make_async_remote_copy(
-            src_ref=rows.at[place_of(*there)],
-            dst_ref=landed.at[me],
+            src_ref=row_of(there),
+            dst_ref=landed,
             send_sem=send_sem,
             recv_sem=recv_sem,
             device_id=target_of(*there),
             device_id_type=MESH,
         ).start()
 
-    for_all_others(send)
-
-
-def await_rows(rows, landed, sem):
-    pltpu.make_async_copy(rows, landed, sem).wait()
+    for_others(half, send)
+
+
+def await_bytes(like, sem):
+    pltpu.make_async_copy(like, like, sem).wait()
 
 
 def label_copies(stage, all_labels, send_sems, recv_sems):
     z, y, x, core = here()
-    if stage == 0:
-        part = all_labels.at[core, x, y, z]
-        peers = [(lax.rem(z + k, 8), y, x, core) for k in range(1, 8)]
-        first = 0
-    elif stage == 1:
-        part = all_labels.at[core, x, y]
-        peers = [(z, lax.rem(y + k, 4), x, core) for k in range(1, 4)]
-        first = 7
-    elif stage == 2:
-        part = all_labels.at[core, x]
-        peers = [(z, y, lax.rem(x + k, 4), core) for k in range(1, 4)]
-        first = 10
-    else:
-        part = all_labels.at[core]
-        peers = [(z, y, x, 1 - core)]
-        first = 13
+    part = (
+        all_labels.at[core, x, y, z],
+        all_labels.at[core, x, y],
+        all_labels.at[core, x],
+        all_labels.at[core],
+    )[stage]
+    first = (0, 7, 10, 13)[stage]
+    peers = lines()[stage]
     return [
         pltpu.make_async_remote_copy(
             src_ref=part,
@@ -330,14 +318,19 @@
     mesh_rows,
     sent,
     arrived,
-    rows_t,
+    rows_high,
+    rows_low,
     labels_t,
+    labels_x,
     onehot_y,
     plane,
+    fields,
+    cells,
     replies_t,
     replies,
     returned,
     spare,
+    spare_two,
     lifts,
     kernel,
     field_high,
@@ -351,13 +344,17 @@
     send_two,
     recv_two,
 ):
-    barrier = enter()
+    barrier = pltpu.get_barrier_semaphore()
+    for peers in lines():
+        for peer in peers:
+            pl.semaphore_signal(barrier, inc=1, device_id=target_of(*peer), device_id_type=MESH)
     z, y, x, core = here()
+    low = place_of(z, y, x, 0)
     bin_labels(row_ids, ids_cols, bins_cols)
     for c in range(ROWS // 128):
         part = jnp.transpose(bins_cols[c * 128 : (c + 1) * 128, :])
         own_labels[0:1, c * 128 : (c + 1) * 128] = part[0:1, :]
-    pl.semaphore_wait(barrier, DEVICES - 1)
+    pl.semaphore_wait(barrier, 14)
     mine = pltpu.make_async_copy(own_labels.at[0], all_labels.at[core, x, y, z], sem_own)
     mine.start()
     mine.wait()
@@ -374,7 +371,6 @@
     corners(slots, ids_cols, corner)
     class_weights(corner, fractions, tab_x, tab_y, True)
     class_weights_z(stencil_z, fractions, tab_z, True)
-    labels_on(1)
     for c in range(ATOMS // CHUNK):
         lanes = slice(c * CHUNK, (c + 1) * CHUNK)
         pre, sigma, out_w = hidden(features, w_in, w_out, lanes)
@@ -382,7 +378,7 @@
         atom = lax.broadcasted_iota(jnp.int32, (1, CHUNK), 1) + c * CHUNK
         charges[0:1, lanes] = jnp.where(atom < atom_count[0], charge, 0.0)
         lifts[:, lanes] = (sigma * (1.0 + pre * (1.0 - sigma)) * out_w).astype(BF16)
-    labels_on(2)
+    labels_on(1)
     for c in range(ATOMS // CHUNK):
         lanes = slice(c * CHUNK, (c + 1) * CHUNK)
         row_weights(tab_x, tab_y, bins_cols, lanes, [weights.at[k, c] for k in range(2)], 0, 1)
@@ -404,51 +400,75 @@
             mesh_rows[...] = total
         else:
             mesh_rows[...] += total
-        if c == 1:
-            labels_on(3)
+        if c in (0, 2):
+            labels_on(2 + c // 2)
     sent[...] = dot3((basis[0], basis[1]), split(mesh_rows[...]))
-    send_rows(sent, arrived, spare, send_one, recv_one)
     labels_on(4)
-
-    blocks = DEVICES // 2
-    for b in range(2):
+    own = sent.at[core * 128 + low]
+    pltpu.make_async_copy(own, arrived.at[0, low], recv_one.at[0]).start()
+    pltpu.make_async_copy(own, spare, send_one).start()
+    for half in range(2):
+        send_half(
+            half,
+            lambda there: sent.at[place_of(*there)],
+            arrived.at[half, low],
+            send_one,
+            recv_one.at[half],
+        )
+
+    cell_y = lax.broadcasted_iota(jnp.int32, (32, 128), 0).astype(F32)
+    for half in range(2):
         for c in range(ROWS // 128):
-            part = all_labels[b, :, :, :, c * 128 : (c + 1) * 128].reshape(128, 128)
-            dst = (slice(c * 128, (c + 1) * 128), slice(b * 128, (b + 1) * 128))
-            labels_t[dst] = jnp.transpose(part)
-    cell_y = lax.broadcasted_iota(jnp.int32, (32, GRID), 0).astype(F32)
-
-    @pl.loop(0, 32)
-    def _(xb):
-        for rank in range(2):
-            label = labels_t[pl.ds(pl.multiple_of(rank * 256 + xb * 8, 8), 8), :]
-            label_y = label - 32.0 * jnp.floor(label * (1.0 / 32.0))
-            for yb in range(8):
-                hit = jnp.broadcast_to(label_y[yb : yb + 1], (32, GRID)) == cell_y
-                onehot_y[xb * 8 + yb, :, rank * GRID : (rank + 1) * GRID] = jnp.where(
-                    hit, 1.0, 0.0
-                ).astype(BF16)
+            bins = slice(c * 128, (c + 1) * 128)
+            part = all_labels[lax.rem(core + half, 2), :, :, :, bins].reshape(128, 128)
+            part = jnp.transpose(part)
+            labels_t[half, bins, :] = part.astype(jnp.int32)
+            labels_x[half, bins, :] = jnp.floor(part * (1.0 / 32.0))
+
+        @pl.loop(0, 32)
+        def _(xb):
+            for rank in range(2):
+                at = pl.ds(pl.multiple_of(rank * 256 + xb * 8, 8), 8)
+                label_y = (labels_t[half, at, :] & 31).astype(F32)
+                for yb in range(8):
+                    hit = jnp.broadcast_to(label_y[yb : yb + 1], (32, 128)) == cell_y
+                    onehot_y[half, xb * 8 + yb, :, rank * 128 : (rank + 1) * 128] = jnp.where(
+                        hit, 1.0, 0.0
+                    ).astype(BF16)
 
     for c in range(ATOMS // CHUNK):
         lanes = slice(c * CHUNK, (c + 1) * CHUNK)
         row_weights(tab_x, tab_y, bins_cols, lanes, [weights.at[k, c] for k in range(2, 6)], 1, 3)
-    coulomb(kernel, place_of(z, y, x, core))
-    await_rows(sent, arrived, recv_one)
-
-    for b in range(2):
+    coulomb(kernel, core * 128 + low)
+    for half in range(2):
+        await_bytes(arrived.at[half], recv_one.at[half])
         for c in range(ROWS // 128):
-            src = (slice(b * 128, (b + 1) * 128), slice(c * 128, (c + 1) * 128))
-            dst = (slice(c * 128, (c + 1) * 128), slice(b * 128, (b + 1) * 128))
-            rows_t[dst] = jnp.transpose(arrived[src])
-    solve_plane(rows_t, labels_t, onehot_y, tabs, kernel, plane, replies_t)
-    for b in range(2):
+            bins = slice(c * 128, (c + 1) * 128)
+            part = jnp.transpose(arrived[half, :, bins])
+            part_high = part.astype(BF16).astype(F32)
+            rows_high[half, bins, :] = part_high
+            rows_low[half, bins, :] = part - part_high
+        gather_plane(half, rows_high, rows_low, labels_x, onehot_y, plane)
+    solve_plane(tabs, kernel, plane, fields)
+    spread_cells(fields, cells)
+    own = replies.at[0, low]
+    for half in range(2):
+        answer(half, cells, labels_t, replies_t)
         for c in range(ROWS // 128):
-            src = (slice(c * 128, (c + 1) * 128), slice(b * 128, (b + 1) * 128))
-            dst = (slice(b * 128, (b + 1) * 128), slice(c * 128, (c + 1) * 128))
-            replies[dst] = jnp.transpose(replies_t[src])
-    await_rows(sent, arrived, send_one)
-    send_rows(replies, returned, spare, send_two, recv_two)
-    await_rows(replies, returned, recv_two)
+            bins = slice(c * 128, (c + 1) * 128)
+            replies[half, :, bins] = jnp.transpose(replies_t[half, bins, :])
+        if half == 0:
+            pltpu.make_async_copy(own, returned.at[core * 128 + low], recv_two).start()
+            pltpu.make_async_copy(own, spare_two, send_two).start()
+        send_half(
+            half,
+            lambda there: replies.at[half, place_of(there[0], there[1], there[2], 0)],
+            returned.at[core * 128 + low],
+            send_two,
+            recv_two,
+        )
+    await_bytes(sent, send_one)
+    await_bytes(returned, recv_two)
 
     field_high[...], field_low[...] = split(
         dot3((basis_t[0], basis_t[1]), split(returned[...]))
@@ -477,7 +497,7 @@
         for b in range(CHUNK // 128):
             rows = slice(c * CHUNK + b * 128, c * CHUNK + (b + 1) * 128)
             grads[rows, :] = jnp.transpose(grad[:, b * 128 : (b + 1) * 128]).astype(BF16)
-    await_rows(replies, returned, send_two)
+    await_bytes(returned, send_two)
 
 
 def coulomb(kernel, wave_index):
@@ -496,61 +516,65 @@
     kernel[...] = jnp.where(keep, values, 0.0)
 
 
-def solve_plane(rows_t, labels_t, onehot_y, tabs, kernel, plane, replies_t):
-    lane_class = lax.broadcasted_iota(jnp.int32, (8, GRID), 0).astype(F32)
+def gather_plane(half, rows_high, rows_low, labels_x, onehot_y, plane):
+    lane_class = lax.broadcasted_iota(jnp.int32, (8, 128), 0).astype(F32)
 
     @pl.loop(0, 32)
     def _(xb):
-        groups = []
-        for rank in range(2):
-            at = pl.ds(pl.multiple_of(rank * 256 + xb * 8, 8), 8)
-            value = rows_t[at, :]
-            value_high = value.astype(BF16).astype(F32)
-            label_x = jnp.floor(labels_t[at, :] * (1.0 / 32.0))
-            groups.append((value_high, value - value_high, label_x))
         pieces = []
         for yb in range(8):
-            left = []
-            for value_high, value_low, label_x in groups:
-                hit = jnp.broadcast_to(label_x[yb : yb + 1], (8, GRID)) == lane_class
-                both = [
-                    jnp.where(hit, jnp.broadcast_to(part[yb : yb + 1], (8, GRID)), 0.0)
-                    for part in (value_high, value_low)
-                ]
-                left.append(jnp.concatenate(both, axis=0).astype(BF16))
-            piece = dot(jnp.concatenate(left, axis=1), onehot_y[xb * 8 + yb], NT)
+            high, low = [], []
+            for rank in range(2):
+                at = pl.ds(rank * 256 + xb * 8 + yb, 1)
+                hit = jnp.broadcast_to(labels_x[half, at, :], (8, 128)) == lane_class
+                high.append(jnp.where(hit, jnp.broadcast_to(rows_high[half, at, :], (8, 128)), 0.0))
+                low.append(jnp.where(hit, jnp.broadcast_to(rows_low[half, at, :], (8, 128)), 0.0))
+            left = [jnp.concatenate([high[r], low[r]], axis=0).astype(BF16) for r in range(2)]
+            piece = dot(jnp.concatenate(left, axis=1), onehot_y[half, xb * 8 + yb], NT)
             pieces.append(piece[0:8] + piece[8:16])
-        plane[pl.ds(pl.multiple_of(xb * 8, 8), 8), :] = jnp.concatenate(pieces, axis=1)
-
+        at = pl.ds(pl.multiple_of(xb * 8, 8), 8)
+        total = jnp.concatenate(pieces, axis=1)
+        if half == 0:
+            plane[at, :] = total
+        else:
+            plane[at, :] += total
+
+
+def solve_plane(tabs, kernel, plane, fields):
     along_x, back_x, along_y = [(tabs[2 * k], tabs[2 * k + 1]) for k in range(3)]
     spectrum = dot3(along_x, split(plane[...]))
     spectrum = dot3(split(spectrum), along_y, NT) * kernel[...]
     field = dot3(back_x, split(spectrum))
-    plane[...] = dot3(split(field), along_y)
-
-    upper = lax.broadcasted_iota(jnp.int32, (8, 128), 0) >= 4
-    offset = (lax.broadcasted_iota(jnp.int32, (8, 128), 0) & 3) * 32
-
-    @pl.loop(0, 32)
-    def _(xb):
-        sources = []
-        field_rows = plane[pl.ds(pl.multiple_of(xb * 8, 8), 8), :]
-        for h in range(8):
-            row = jnp.broadcast_to(field_rows[h : h + 1], (8, GRID))
-            sources.append(jnp.where(upper, row[:, 128:], row[:, :128]))
+    field = dot3(split(field), along_y)
+    fields[0] = field[:, :128]
+    fields[1] = field[:, 128:]
+
+
+def spread_cells(fields, cells):
+    block = lax.broadcasted_iota(jnp.int32, (32, 128), 1) // 32
+    for yb in range(8):
+        for h in range(2):
+            chosen = None
+            for q in range(4):
+                part = fields[yb // 4, pl.ds(4 * h + q, 32, stride=8), :]
+                shift = (q - yb % 4) % 4 * 32
+                part = pltpu.roll(part, shift, 1) if shift else part
+                chosen = part if q == 0 else jnp.where(block == q, part, chosen)
+            cells[yb, h] = chosen
+
+
+def answer(half, cells, labels_t, replies_t):
+    for yb in range(8):
         for rank in range(2):
-            at = pl.ds(pl.multiple_of(rank * 256 + xb * 8, 8), 8)
-            for b in range(2):
-                label = labels_t[at, b * 128 : (b + 1) * 128].astype(jnp.int32)
-                label_x = label >> 5
-                index = (label & 31) + offset
-                value = jnp.zeros((8, 128), F32)
-                for h in range(8):
-                    taken = jnp.take_along_axis(
-                        sources[h], index, axis=1, mode="promise_in_bounds"
-                    )
-                    value = jnp.where(label_x == h, taken, value)
-                replies_t[at, b * 128 : (b + 1) * 128] = value
+            at = pl.ds(rank * 256 + yb, 32, stride=8)
+            label = labels_t[half, at, :]
+            index = label & 127
+            upper = label >> 7
+            value = jnp.zeros((32, 128), F32)
+            for h in range(2):
+                taken = jnp.take_along_axis(cells[yb, h], index, axis=1, mode="promise_in_bounds")
+                value = jnp.where(upper == h, taken, value)
+            replies_t[half, at, :] = value
 
 
 VM = pl.BlockSpec(memory_space=pltpu.VMEM)
@@ -583,14 +607,19 @@
             vmem((GRID, CHUNK), BF16),
             vmem((GRID, ROWS), F32),
             vmem((DEVICES, ROWS), F32),
+            vmem((2, 128, ROWS), F32),
+            vmem((2, ROWS, 128), F32),
+            vmem((2, ROWS, 128), F32),
+            vmem((2, ROWS, 128), jnp.int32),
+            vmem((2, ROWS, 128), F32),
+            vmem((2, GRID, 32, 256), BF16),
+            vmem((GRID, GRID), F32),
+            vmem((2, GRID, 128), F32),
+            vmem((8, 2, 32, 128), F32),
+            vmem((2, ROWS, 128), F32),
+            vmem((2, 128, ROWS), F32),
             vmem((DEVICES, ROWS), F32),
-            vmem((ROWS, GRID), F32),
-            vmem((ROWS, GRID), F32),
-            vmem((GRID, 32, 2 * GRID), BF16),
-            vmem((GRID, GRID), F32),
-            vmem((ROWS, GRID), F32),
-            vmem((DEVICES, ROWS), F32),
-            vmem((DEVICES, ROWS), F32),
+            vmem((ROWS,), F32),
             vmem((ROWS,), F32),
             vmem((128, ATOMS), BF16),
             vmem((GRID, GRID), F32),
@@ -600,7 +629,13 @@
             pltpu.SemaphoreType.DMA((14,)),
             pltpu.SemaphoreType.DMA((14,)),
         ]
-        + [pltpu.SemaphoreType.DMA] * 5,
+        + [
+            pltpu.SemaphoreType.DMA,
+            pltpu.SemaphoreType.DMA,
+            pltpu.SemaphoreType.DMA((2,)),
+            pltpu.SemaphoreType.DMA,
+            pltpu.SemaphoreType.DMA,
+        ],
         compiler_params=pltpu.CompilerParams(
             vmem_limit_bytes=VMEM_LIMIT, collective_id=0, has_side_effects=True
         ),

time: 86.1 us -> 79.8 us (0.927)
  Pallas kernels: 81.4 us -> 75.1 us
    pallas_call x1, Pallas kernels: 81.4 us -> 75.1 us  [local(): pl.pallas_call(step_kernel, out_shape=(jax.ShapeDtypeStruct((3, ATOMS), F...]
where the time goes in v3:
time: 79.8 us; the launch traced here: 79.6 us
  Pallas kernels  75.1 us (94%)
  local copies, waits for them, and re-layouts  3.25 us (4%)
  between operations  1.29 us (2%)
    pallas_call x1, Pallas kernels, local(): pl.pallas_call(step_kernel, out_shape=(jax.ShapeDtypeStruct((3, ATOMS), F...  75.1 us
    unnamed x2, local copies, waits for them, and re-layouts  3.25 us

profile of v3, /device:TPU:1, one launch (start us, length us, event | category | flops | bytes accessed | tf_op | source)
XLA Modules:
  0.0 79.6 jit_solution(12990037393341079142)
XLA Ops:
  1.3 75.1 %step.1 = (f32[3,2048]{1,0:T(4,128)}, bf16[2048,128]{1,0:T(8,128)(2,1)}) custom-call(s32[1,512]{1,0:T(1,128)} %row_ids.1, s32[16,2048]{1,0:T(8,128)} %slots.1, s32[1,2048]{1,0:T(1,128)} %bitcast.2, f32[3,2048]{1,0:T(4,128)} %fractions.1, s32[1]{0:T(128)S(6)} %copy.15.atom_count, bf16[2048,128]{1,0:T(8,128)(2,1)} %features.1, bf16[128,128]{1,0:T(8,128)(2,1)} %w_in.1, ...), custom_call_target="tpu_custom_call" | custom-call | tf_op jit(solution)/shard_map/step/pallas_call | solution.py:588
  76.3 1.4 %copy.16 = f32[3,2048]{1,0:T(4,128)} copy(f32[3,2048]{1,0:T(4,128)} %get-tuple-element.4) | data formatting | bytes 49152
  77.7 1.9 %copy.17 = bf16[2048,128]{1,0:T(8,128)(2,1)} copy(bf16[2048,128]{1,0:T(8,128)(2,1)} %get-tuple-element.5) | data formatting | bytes 1048576

commit v4 on v3

--- a/solution.py
+++ b/solution.py
@@ -323,6 +323,7 @@
     labels_t,
     labels_x,
     onehot_y,
+    crossed,
     plane,
     fields,
     cells,
@@ -338,6 +339,7 @@
     weights,
     label_send,
     label_recv,
+    line_sems,
     sem_own,
     send_one,
     recv_one,
@@ -367,6 +369,16 @@
             for copy in label_copies(stage, all_labels, label_send, label_recv):
                 copy.start()
 
+    def heard_from(stage):
+        if stage > 0:
+            pl.semaphore_wait(line_sems.at[stage - 1], (3, 3, 1)[stage - 1])
+        if stage < 3:
+            for peer in lines()[stage + 1]:
+                pl.semaphore_signal(
+                    line_sems.at[stage], inc=1, device_id=target_of(*peer), device_id_type=MESH
+                )
+
+    heard_from(0)
     labels_on(0)
     corners(slots, ids_cols, corner)
     class_weights(corner, fractions, tab_x, tab_y, True)
@@ -378,6 +390,7 @@
         atom = lax.broadcasted_iota(jnp.int32, (1, CHUNK), 1) + c * CHUNK
         charges[0:1, lanes] = jnp.where(atom < atom_count[0], charge, 0.0)
         lifts[:, lanes] = (sigma * (1.0 + pre * (1.0 - sigma)) * out_w).astype(BF16)
+    heard_from(1)
     labels_on(1)
     for c in range(ATOMS // CHUNK):
         lanes = slice(c * CHUNK, (c + 1) * CHUNK)
@@ -400,10 +413,11 @@
             mesh_rows[...] = total
         else:
             mesh_rows[...] += total
-        if c in (0, 2):
-            labels_on(2 + c // 2)
+        if c == 1:
+            heard_from(2)
+            labels_on(2)
     sent[...] = dot3((basis[0], basis[1]), split(mesh_rows[...]))
-    labels_on(4)
+    heard_from(3)
     own = sent.at[core * 128 + low]
     pltpu.make_async_copy(own, arrived.at[0, low], recv_one.at[0]).start()
     pltpu.make_async_copy(own, spare, send_one).start()
@@ -415,7 +429,13 @@
             send_one,
             recv_one.at[half],
         )
-
+        if half == 0:
+            labels_on(3)
+    for c in range(ATOMS // CHUNK):
+        lanes = slice(c * CHUNK, (c + 1) * CHUNK)
+        row_weights(tab_x, tab_y, bins_cols, lanes, [weights.at[k, c] for k in range(2, 6)], 1, 3)
+    coulomb(kernel, core * 128 + low)
+    labels_on(4)
     cell_y = lax.broadcasted_iota(jnp.int32, (32, 128), 0).astype(F32)
     for half in range(2):
         for c in range(ROWS // 128):
@@ -432,14 +452,10 @@
                 label_y = (labels_t[half, at, :] & 31).astype(F32)
                 for yb in range(8):
                     hit = jnp.broadcast_to(label_y[yb : yb + 1], (32, 128)) == cell_y
-                    onehot_y[half, xb * 8 + yb, :, rank * 128 : (rank + 1) * 128] = jnp.where(
+                    onehot_y[half, xb, yb * 32 : yb * 32 + 32, rank * 128 : rank * 128 + 128] = jnp.where(
                         hit, 1.0, 0.0
                     ).astype(BF16)
 
-    for c in range(ATOMS // CHUNK):
-        lanes = slice(c * CHUNK, (c + 1) * CHUNK)
-        row_weights(tab_x, tab_y, bins_cols, lanes, [weights.at[k, c] for k in range(2, 6)], 1, 3)
-    coulomb(kernel, core * 128 + low)
     for half in range(2):
         await_bytes(arrived.at[half], recv_one.at[half])
         for c in range(ROWS // 128):
@@ -448,7 +464,8 @@
             part_high = part.astype(BF16).astype(F32)
             rows_high[half, bins, :] = part_high
             rows_low[half, bins, :] = part - part_high
-        gather_plane(half, rows_high, rows_low, labels_x, onehot_y, plane)
+        gather_plane(half, rows_high, rows_low, labels_x, onehot_y, crossed)
+    keep_matching(crossed, plane)
     solve_plane(tabs, kernel, plane, fields)
     spread_cells(fields, cells)
     own = replies.at[0, low]
@@ -516,28 +533,37 @@
     kernel[...] = jnp.where(keep, values, 0.0)
 
 
-def gather_plane(half, rows_high, rows_low, labels_x, onehot_y, plane):
-    lane_class = lax.broadcasted_iota(jnp.int32, (8, 128), 0).astype(F32)
-
+def gather_plane(half, rows_high, rows_low, labels_x, onehot_y, crossed):
     @pl.loop(0, 32)
     def _(xb):
-        pieces = []
-        for yb in range(8):
-            high, low = [], []
-            for rank in range(2):
-                at = pl.ds(rank * 256 + xb * 8 + yb, 1)
-                hit = jnp.broadcast_to(labels_x[half, at, :], (8, 128)) == lane_class
-                high.append(jnp.where(hit, jnp.broadcast_to(rows_high[half, at, :], (8, 128)), 0.0))
-                low.append(jnp.where(hit, jnp.broadcast_to(rows_low[half, at, :], (8, 128)), 0.0))
-            left = [jnp.concatenate([high[r], low[r]], axis=0).astype(BF16) for r in range(2)]
-            piece = dot(jnp.concatenate(left, axis=1), onehot_y[half, xb * 8 + yb], NT)
-            pieces.append(piece[0:8] + piece[8:16])
-        at = pl.ds(pl.multiple_of(xb * 8, 8), 8)
-        total = jnp.concatenate(pieces, axis=1)
+        left = []
+        for rank in range(2):
+            at = pl.ds(pl.multiple_of(rank * 256 + xb * 8, 8), 8)
+            high, low = rows_high[half, at, :], rows_low[half, at, :]
+            label_x = labels_x[half, at, :]
+            hits = [label_x == float(h) for h in range(8)]
+            parts = [jnp.where(hit, part, 0.0) for part in (high, low) for hit in hits]
+            left.append(jnp.concatenate(parts, axis=0).astype(BF16))
+        both = dot(jnp.concatenate(left, axis=1), onehot_y[half, xb], NT)
+        total = both[0:64] + both[64:128]
         if half == 0:
-            plane[at, :] = total
+            crossed[xb] = total
         else:
-            plane[at, :] += total
+            crossed[xb] += total
+
+
+def keep_matching(crossed, plane):
+    lane_class = lax.broadcasted_iota(jnp.int32, (8, GRID), 1) // 32
+    match = lane_class == lax.broadcasted_iota(jnp.int32, (8, GRID), 0)
+    row = lax.broadcasted_iota(jnp.int32, (8, GRID), 0)
+
+    @pl.loop(0, 32)
+    def _(xb):
+        total = jnp.zeros((8, GRID), F32)
+        for h in range(8):
+            part = jnp.where(match, crossed[xb, h * 8 : h * 8 + 8, :], 0.0)
+            total = jnp.where(row == h, jnp.sum(part, axis=0, keepdims=True), total)
+        plane[pl.ds(pl.multiple_of(xb * 8, 8), 8), :] = total
 
 
 def solve_plane(tabs, kernel, plane, fields):
@@ -612,7 +638,8 @@
             vmem((2, ROWS, 128), F32),
             vmem((2, ROWS, 128), jnp.int32),
             vmem((2, ROWS, 128), F32),
-            vmem((2, GRID, 32, 256), BF16),
+            vmem((2, 32, GRID, 256), BF16),
+            vmem((32, 64, GRID), F32),
             vmem((GRID, GRID), F32),
             vmem((2, GRID, 128), F32),
             vmem((8, 2, 32, 128), F32),
@@ -628,6 +655,7 @@
             vmem((6, chunks, ROWS, CHUNK), BF16),
             pltpu.SemaphoreType.DMA((14,)),
             pltpu.SemaphoreType.DMA((14,)),
+            pltpu.SemaphoreType.REGULAR((3,)),
         ]
         + [
             pltpu.SemaphoreType.DMA,

time: 79.8 us -> 72.8 us (0.912)
  Pallas kernels: 75.1 us -> 68 us
    pallas_call x1, Pallas kernels: 75.1 us -> 68 us  [local(): pl.pallas_call(step_kernel, out_shape=(jax.ShapeDtypeStruct((3, ATOMS), F...]
where the time goes in v4:
time: 72.8 us; the launch traced here: 72.6 us
  Pallas kernels  68 us (93%)
  local copies, waits for them, and re-layouts  3.25 us (4%)
  between operations  1.29 us (2%)
    pallas_call x1, Pallas kernels, local(): pl.pallas_call(step_kernel, out_shape=(jax.ShapeDtypeStruct((3, ATOMS), F...  68 us
    unnamed x2, local copies, waits for them, and re-layouts  3.25 us

profile of v4, /device:TPU:1, one launch (start us, length us, event | category | flops | bytes accessed | tf_op | source)
XLA Modules:
  0.0 72.6 jit_solution(6743766134649464848)
XLA Ops:
  1.3 68.0 %step.1 = (f32[3,2048]{1,0:T(4,128)}, bf16[2048,128]{1,0:T(8,128)(2,1)}) custom-call(s32[1,512]{1,0:T(1,128)} %row_ids.1, s32[16,2048]{1,0:T(8,128)} %slots.1, s32[1,2048]{1,0:T(1,128)} %bitcast.2, f32[3,2048]{1,0:T(4,128)} %fractions.1, s32[1]{0:T(128)S(6)} %copy.15.atom_count, bf16[2048,128]{1,0:T(8,128)(2,1)} %features.1, bf16[128,128]{1,0:T(8,128)(2,1)} %w_in.1, ...), custom_call_target="tpu_custom_call" | custom-call | tf_op jit(solution)/shard_map/step/pallas_call | solution.py:614
  69.3 1.4 %copy.16 = f32[3,2048]{1,0:T(4,128)} copy(f32[3,2048]{1,0:T(4,128)} %get-tuple-element.4) | data formatting | bytes 49152
  70.7 1.9 %copy.17 = bf16[2048,128]{1,0:T(8,128)(2,1)} copy(bf16[2048,128]{1,0:T(8,128)(2,1)} %get-tuple-element.5) | data formatting | bytes 1048576

commit v5 on v4

--- a/solution.py
+++ b/solution.py
@@ -17,6 +17,9 @@
 ATOMS = 2048
 DEVICES = 256
 CHUNK = 512
+UNROLL = 8
+UNROLL_W = 2
+UNROLL_Y = 4
 VMEM_LIMIT = 56 * 1024 * 1024
 F32 = jnp.float32
 BF16 = jnp.bfloat16
@@ -180,8 +183,7 @@
         rows = [tab_x[index, pl.ds(2 * i + k, 1), lanes] for k in range(2)]
         return jnp.concatenate([jnp.broadcast_to(row, (8, width)) for row in rows], axis=0)
 
-    @pl.loop(0, 16)
-    def _(i):
+    def one(i):
         wx = pair(0, i)
         key = pair(1, i) + ky
         values = [wx * wy, pair(2, i) * wy, wx * sy][first:last]
@@ -194,6 +196,11 @@
                 high, low = split(jnp.where(hit, value, 0.0))
                 outs[2 * k][rows, :] = high
                 outs[2 * k + 1][rows, :] = low
+
+    @pl.loop(0, 16 // UNROLL_W)
+    def _(step):
+        for k in range(UNROLL_W):
+            one(step * UNROLL_W + k)
 
 
 def hidden(features, w_in, w_out, lanes):
@@ -445,9 +452,10 @@
             labels_t[half, bins, :] = part.astype(jnp.int32)
             labels_x[half, bins, :] = jnp.floor(part * (1.0 / 32.0))
 
-        @pl.loop(0, 32)
-        def _(xb):
-            for rank in range(2):
+        @pl.loop(0, 32 // UNROLL_Y)
+        def _(step):
+            for k, rank in [(k, rank) for k in range(UNROLL_Y) for rank in range(2)]:
+                xb = step * UNROLL_Y + k
                 at = pl.ds(pl.multiple_of(rank * 256 + xb * 8, 8), 8)
                 label_y = (labels_t[half, at, :] & 31).astype(F32)
                 for yb in range(8):
@@ -534,8 +542,7 @@
 
 
 def gather_plane(half, rows_high, rows_low, labels_x, onehot_y, crossed):
-    @pl.loop(0, 32)
-    def _(xb):
+    def one(xb):
         left = []
         for rank in range(2):
             at = pl.ds(pl.multiple_of(rank * 256 + xb * 8, 8), 8)
@@ -545,11 +552,16 @@
             parts = [jnp.where(hit, part, 0.0) for part in (high, low) for hit in hits]
             left.append(jnp.concatenate(parts, axis=0).astype(BF16))
         both = dot(jnp.concatenate(left, axis=1), onehot_y[half, xb], NT)
-        total = both[0:64] + both[64:128]
-        if half == 0:
-            crossed[xb] = total
-        else:
-            crossed[xb] += total
+        return both[0:64] + both[64:128]
+
+    @pl.loop(0, 32 // UNROLL)
+    def _(step):
+        totals = [one(step * UNROLL + k) for k in range(UNROLL)]
+        for k, total in enumerate(totals):
+            if half == 0:
+                crossed[step * UNROLL + k] = total
+            else:
+                crossed[step * UNROLL + k] += total
 
 
 def keep_matching(crossed, plane):
@@ -557,13 +569,15 @@
     match = lane_class == lax.broadcasted_iota(jnp.int32, (8, GRID), 0)
     row = lax.broadcasted_iota(jnp.int32, (8, GRID), 0)
 
-    @pl.loop(0, 32)
-    def _(xb):
-        total = jnp.zeros((8, GRID), F32)
-        for h in range(8):
-            part = jnp.where(match, crossed[xb, h * 8 : h * 8 + 8, :], 0.0)
-            total = jnp.where(row == h, jnp.sum(part, axis=0, keepdims=True), total)
-        plane[pl.ds(pl.multiple_of(xb * 8, 8), 8), :] = total
+    @pl.loop(0, 8)
+    def _(step):
+        for k in range(4):
+            xb = step * 4 + k
+            total = jnp.zeros((8, GRID), F32)
+            for h in range(8):
+                part = jnp.where(match, crossed[xb, h * 8 : h * 8 + 8, :], 0.0)
+                total = jnp.where(row == h, jnp.sum(part, axis=0, keepdims=True), total)
+            plane[pl.ds(pl.multiple_of(xb * 8, 8), 8), :] = total
 
 
 def solve_plane(tabs, kernel, plane, fields):

time: 72.8 us -> 67.6 us (0.929)
  Pallas kernels: 68 us -> 62.8 us
    pallas_call x1, Pallas kernels: 68 us -> 62.8 us  [local(): pl.pallas_call(step_kernel, out_shape=(jax.ShapeDtypeStruct((3, ATOMS), F...]
where the time goes in v5:
time: 67.6 us; the launch traced here: 67.3 us
  Pallas kernels  62.8 us (93%)
  local copies, waits for them, and re-layouts  3.25 us (5%)
  between operations  1.29 us (2%)
    pallas_call x1, Pallas kernels, local(): pl.pallas_call(step_kernel, out_shape=(jax.ShapeDtypeStruct((3, ATOMS), F...  62.8 us
    unnamed x2, local copies, waits for them, and re-layouts  3.25 us

profile of v5, /device:TPU:1, one launch (start us, length us, event | category | flops | bytes accessed | tf_op | source)
XLA Modules:
  0.0 67.3 jit_solution(12265634773434469113)
XLA Ops:
  1.3 62.8 %step.1 = (f32[3,2048]{1,0:T(4,128)}, bf16[2048,128]{1,0:T(8,128)(2,1)}) custom-call(s32[1,512]{1,0:T(1,128)} %row_ids.1, s32[16,2048]{1,0:T(8,128)} %slots.1, s32[1,2048]{1,0:T(1,128)} %bitcast.2, f32[3,2048]{1,0:T(4,128)} %fractions.1, s32[1]{0:T(128)S(6)} %copy.15.atom_count, bf16[2048,128]{1,0:T(8,128)(2,1)} %features.1, bf16[128,128]{1,0:T(8,128)(2,1)} %w_in.1, ...), custom_call_target="tpu_custom_call" | custom-call | tf_op jit(solution)/shard_map/step/pallas_call | solution.py:628
  64.1 1.4 %copy.16 = f32[3,2048]{1,0:T(4,128)} copy(f32[3,2048]{1,0:T(4,128)} %get-tuple-element.4) | data formatting | bytes 49152
  65.5 1.9 %copy.17 = bf16[2048,128]{1,0:T(8,128)(2,1)} copy(bf16[2048,128]{1,0:T(8,128)(2,1)} %get-tuple-element.5) | data formatting | bytes 1048576

commit v6 on v5

--- a/solution.py
+++ b/solution.py
@@ -170,7 +170,7 @@
         tab_z[16:24, :] = pick(step_z, spline_slopes(fractions[2:3, :]))
 
 
-def row_weights(tab_x, tab_y, bins_cols, lanes, outs, first, last):
+def row_weights(tab_x, tab_y, bins_cols, lanes, outs, last, step):
     def twice(part):
         return jnp.concatenate([part, part], axis=0)
 
@@ -186,7 +186,7 @@
     def one(i):
         wx = pair(0, i)
         key = pair(1, i) + ky
-        values = [wx * wy, pair(2, i) * wy, wx * sy][first:last]
+        values = [wx * wy, pair(2, i) * wy, wx * sy][:last]
         for rank in range(2):
             rows = pl.ds(pl.multiple_of(rank * 256 + i * 16, 16), 16)
             label = bins_cols[rows, :]
@@ -194,22 +194,14 @@
             hit = key == label
             for k, value in enumerate(values):
                 high, low = split(jnp.where(hit, value, 0.0))
-                outs[2 * k][rows, :] = high
-                outs[2 * k + 1][rows, :] = low
+                outs[step * k][rows, :] = high
+                if step == 2:
+                    outs[step * k + 1][rows, :] = low
 
     @pl.loop(0, 16 // UNROLL_W)
-    def _(step):
+    def _(block):
         for k in range(UNROLL_W):
-            one(step * UNROLL_W + k)
-
-
-def hidden(features, w_in, w_out, lanes):
-    w_in_t = jnp.transpose(w_in[...].astype(F32)).astype(BF16)
-    pre = dot(w_in_t, features[lanes, :], NT)
-    sigma = jax.nn.sigmoid(pre)
-    out_w = row_to_columns(w_out[...])
-    out_w = jnp.concatenate([out_w] * (pre.shape[1] // 128), axis=1)
-    return (pre, sigma, out_w)
+            one(block * UNROLL_W + k)
 
 
 MESH = pl.DeviceIdType.MESH
@@ -309,8 +301,8 @@
     basis,
     basis_t,
     tabs,
-    forces,
-    grads,
+    sums,
+    lifts,
     ids_cols,
     bins_cols,
     own_labels,
@@ -339,7 +331,6 @@
     returned,
     spare,
     spare_two,
-    lifts,
     kernel,
     field_high,
     field_low,
@@ -390,9 +381,12 @@
     corners(slots, ids_cols, corner)
     class_weights(corner, fractions, tab_x, tab_y, True)
     class_weights_z(stencil_z, fractions, tab_z, True)
+    w_in_t = jnp.transpose(w_in[...].astype(F32)).astype(BF16)
+    out_w = jnp.concatenate([row_to_columns(w_out[...])] * (CHUNK // 128), axis=1)
     for c in range(ATOMS // CHUNK):
         lanes = slice(c * CHUNK, (c + 1) * CHUNK)
-        pre, sigma, out_w = hidden(features, w_in, w_out, lanes)
+        pre = dot(w_in_t, features[lanes, :], NT)
+        sigma = jax.nn.sigmoid(pre)
         charge = jnp.sum(pre * sigma * out_w, axis=0, keepdims=True)
         atom = lax.broadcasted_iota(jnp.int32, (1, CHUNK), 1) + c * CHUNK
         charges[0:1, lanes] = jnp.where(atom < atom_count[0], charge, 0.0)
@@ -401,7 +395,7 @@
     labels_on(1)
     for c in range(ATOMS // CHUNK):
         lanes = slice(c * CHUNK, (c + 1) * CHUNK)
-        row_weights(tab_x, tab_y, bins_cols, lanes, [weights.at[k, c] for k in range(2)], 0, 1)
+        row_weights(tab_x, tab_y, bins_cols, lanes, [weights.at[0, c]], 1, 1)
         key = tab_z[8:16, lanes]
         amount = tab_z[0:8, lanes] * charges[0:1, lanes]
         amount_high = amount.astype(BF16).astype(F32)
@@ -415,7 +409,7 @@
             z_low[rows, :] = jnp.concatenate(
                 [jnp.where(hit, amount_low, 0.0) for hit in hits], axis=0
             ).astype(BF16)
-        total = dot3((z_high[...], z_low[...]), (weights[0, c], weights[1, c]), NT)
+        total = dot(z_high[...], weights[0, c], NT) + dot(z_low[...], weights[0, c], NT)
         if c == 0:
             mesh_rows[...] = total
         else:
@@ -440,7 +434,7 @@
             labels_on(3)
     for c in range(ATOMS // CHUNK):
         lanes = slice(c * CHUNK, (c + 1) * CHUNK)
-        row_weights(tab_x, tab_y, bins_cols, lanes, [weights.at[k, c] for k in range(2, 6)], 1, 3)
+        row_weights(tab_x, tab_y, bins_cols, lanes, [weights.at[k, c] for k in range(6)], 3, 2)
     coulomb(kernel, core * 128 + low)
     labels_on(4)
     cell_y = lax.broadcasted_iota(jnp.int32, (32, 128), 0).astype(F32)
@@ -501,7 +495,7 @@
     for c in range(ATOMS // CHUNK):
         lanes = slice(c * CHUNK, (c + 1) * CHUNK)
         key = tab_z[8:16, lanes]
-        sums = []
+        picked = []
         for k in range(3):
             total = dot3(
                 (field_high[...], field_low[...]), (weights[2 * k, c], weights[2 * k + 1, c])
@@ -509,20 +503,26 @@
             chosen = jnp.zeros((8, CHUNK), F32)
             for h in range(32):
                 chosen = jnp.where(key == float(h), total[h * 8 : (h + 1) * 8], chosen)
-            sums.append(chosen)
+            picked.append(chosen)
         wz = tab_z[0:8, lanes]
-        potential = jnp.sum(wz * sums[0], axis=0, keepdims=True)
+        potential = jnp.sum(wz * picked[0], axis=0, keepdims=True)
         charge = -charges[0:1, lanes]
-        forces[0:1, lanes] = charge * jnp.sum(wz * sums[1], axis=0, keepdims=True)
-        forces[1:2, lanes] = charge * jnp.sum(wz * sums[2], axis=0, keepdims=True)
-        forces[2:3, lanes] = charge * jnp.sum(tab_z[16:24, lanes] * sums[0], axis=0, keepdims=True)
+        sums[0:1, lanes] = charge * jnp.sum(wz * picked[1], axis=0, keepdims=True)
+        sums[1:2, lanes] = charge * jnp.sum(wz * picked[2], axis=0, keepdims=True)
+        sums[2:3, lanes] = charge * jnp.sum(tab_z[16:24, lanes] * picked[0], axis=0, keepdims=True)
         atom = lax.broadcasted_iota(jnp.int32, (1, CHUNK), 1) + c * CHUNK
-        potential = jnp.where(atom < atom_count[0], potential, 0.0)
-        grad = potential * dot(w_in[...], lifts[:, lanes])
+        sums[3:4, lanes] = jnp.where(atom < atom_count[0], potential, 0.0)
+    await_bytes(returned, send_two)
+
+
+def finish_kernel(sums, lifts, w_in, forces, grads):
+    forces[...] = sums[0:3, :]
+    for c in range(ATOMS // CHUNK):
+        lanes = slice(c * CHUNK, (c + 1) * CHUNK)
+        grad = sums[3:4, lanes] * dot(w_in[...], lifts[:, lanes])
         for b in range(CHUNK // 128):
             rows = slice(c * CHUNK + b * 128, c * CHUNK + (b + 1) * 128)
             grads[rows, :] = jnp.transpose(grad[:, b * 128 : (b + 1) * 128]).astype(BF16)
-    await_bytes(returned, send_two)
 
 
 def coulomb(kernel, wave_index):
@@ -625,11 +625,11 @@
     basis, basis_t, plane = [jnp.asarray(table) for table in tables()]
     vmem = pltpu.VMEM
     chunks = ATOMS // CHUNK
-    return pl.pallas_call(
+    sums, lifts = pl.pallas_call(
         step_kernel,
         out_shape=(
-            jax.ShapeDtypeStruct((3, ATOMS), F32),
-            jax.ShapeDtypeStruct((ATOMS, 128), BF16),
+            jax.ShapeDtypeStruct((8, ATOMS), F32),
+            jax.ShapeDtypeStruct((128, ATOMS), BF16),
         ),
         in_specs=[VM] * 4 + [SM] + [VM] * 6,
         out_specs=(VM, VM),
@@ -662,7 +662,6 @@
             vmem((DEVICES, ROWS), F32),
             vmem((ROWS,), F32),
             vmem((ROWS,), F32),
-            vmem((128, ATOMS), BF16),
             vmem((GRID, GRID), F32),
             vmem((GRID, ROWS), BF16),
             vmem((GRID, ROWS), BF16),
@@ -695,6 +694,17 @@
         basis_t,
         plane,
     )
+    return pl.pallas_call(
+        finish_kernel,
+        out_shape=(
+            jax.ShapeDtypeStruct((3, ATOMS), F32),
+            jax.ShapeDtypeStruct((ATOMS, 128), BF16),
+        ),
+        in_specs=[VM] * 3,
+        out_specs=(VM, VM),
+        compiler_params=pltpu.CompilerParams(vmem_limit_bytes=VMEM_LIMIT),
+        name="finish",
+    )(sums, lifts, w_in)
 
 
 def solution(mesh):

time: 67.6 us -> 65.7 us (0.972)
  local copies, waits for them, and re-layouts: 3.25 us -> 0 us
  Pallas kernels: 62.8 us -> 64.3 us
    unnamed x2 -> x0, local copies, waits for them, and re-layouts: 3.25 us -> none
    pallas_call x1 -> x2, Pallas kernels: 62.8 us -> 64.3 us  [the longest x1 62.1 us: local(): pl.pallas_call(step_kernel, out_shape=(jax.ShapeDtypeStruct((8, ATOMS), F...]
where the time goes in v6:
time: 65.7 us; the launch traced here: 65.6 us
  Pallas kernels  64.3 us (98%)
  between operations  1.29 us (2%)
    pallas_call x1, Pallas kernels, local(): pl.pallas_call(step_kernel, out_shape=(jax.ShapeDtypeStruct((8, ATOMS), F...  62.1 us
    pallas_call x1, Pallas kernels, local(): pl.pallas_call(finish_kernel, out_shape=(jax.ShapeDtypeStruct((3, ATOMS),...  2.19 us

profile of v6, /device:TPU:1, one launch (start us, length us, event | category | flops | bytes accessed | tf_op | source)
XLA Modules:
  0.0 65.6 jit_solution(18287677813235325774)
XLA Ops:
  1.3 62.1 %step.1 = (f32[8,2048]{1,0:T(8,128)}, bf16[128,2048]{1,0:T(8,128)(2,1)}) custom-call(s32[1,512]{1,0:T(1,128)} %row_ids.1, s32[16,2048]{1,0:T(8,128)} %slots.1, s32[1,2048]{1,0:T(1,128)} %bitcast.2, f32[3,2048]{1,0:T(4,128)} %fractions.1, s32[1]{0:T(128)S(6)} %copy.13.atom_count, bf16[2048,128]{1,0:T(8,128)(2,1)} %features.1, bf16[128,128]{1,0:T(8,128)(2,1)} %w_in.3, ...), custom_call_target="tpu_custom_call" | custom-call | tf_op jit(solution)/shard_map/step/pallas_call | solution.py:628
  63.4 2.2 %finish.1 = (f32[3,2048]{1,0:T(4,128)}, bf16[2048,128]{1,0:T(8,128)(2,1)}) custom-call(f32[8,2048]{1,0:T(8,128)} %get-tuple-element.4.sums, bf16[128,2048]{1,0:T(8,128)(2,1)} %get-tuple-element.5.lifts, bf16[128,128]{1,0:T(8,128)(2,1)} %w_in.3), custom_call_target="tpu_custom_call" | custom-call | tf_op jit(solution)/shard_map/finish/pallas_call | solution.py:697

commit v7 on v6

--- a/solution.py
+++ b/solution.py
@@ -198,6 +198,10 @@
                 if step == 2:
                     outs[step * k + 1][rows, :] = low
 
+    return one
+
+
+def run_all(one):
     @pl.loop(0, 16 // UNROLL_W)
     def _(block):
         for k in range(UNROLL_W):
@@ -222,7 +226,7 @@
     return (z * 4 + y, x * 2 + core)
 
 
-def for_others(half, visit):
+def for_others(half, visit, beside):
     z, y, x, core = here()
     other_core = lax.rem(core + half, 2)
 
@@ -236,6 +240,8 @@
                 pl.when(k > 0)(functools.partial(visit, there))
             else:
                 visit(there)
+        for work in beside:
+            work(k)
 
 
 def lines():
@@ -248,7 +254,7 @@
     )
 
 
-def send_half(half, row_of, landed, send_sem, recv_sem):
+def send_half(half, row_of, landed, send_sem, recv_sem, beside=()):
     def send(there):
         pltpu.make_async_remote_copy(
             src_ref=row_of(there),
@@ -259,7 +265,7 @@
             device_id_type=MESH,
         ).start()
 
-    for_others(half, send)
+    for_others(half, send, beside)
 
 
 def await_bytes(like, sem):
@@ -395,7 +401,7 @@
     labels_on(1)
     for c in range(ATOMS // CHUNK):
         lanes = slice(c * CHUNK, (c + 1) * CHUNK)
-        row_weights(tab_x, tab_y, bins_cols, lanes, [weights.at[0, c]], 1, 1)
+        run_all(row_weights(tab_x, tab_y, bins_cols, lanes, [weights.at[0, c]], 1, 1))
         key = tab_z[8:16, lanes]
         amount = tab_z[0:8, lanes] * charges[0:1, lanes]
         amount_high = amount.astype(BF16).astype(F32)
@@ -429,12 +435,21 @@
             arrived.at[half, low],
             send_one,
             recv_one.at[half],
+            [
+                row_weights(
+                    tab_x,
+                    tab_y,
+                    bins_cols,
+                    slice(c * CHUNK, (c + 1) * CHUNK),
+                    [weights.at[k, c] for k in range(6)],
+                    3,
+                    2,
+                )
+                for c in (2 * half, 2 * half + 1)
+            ],
         )
         if half == 0:
             labels_on(3)
-    for c in range(ATOMS // CHUNK):
-        lanes = slice(c * CHUNK, (c + 1) * CHUNK)
-        row_weights(tab_x, tab_y, bins_cols, lanes, [weights.at[k, c] for k in range(6)], 3, 2)
     coulomb(kernel, core * 128 + low)
     labels_on(4)
     cell_y = lax.broadcasted_iota(jnp.int32, (32, 128), 0).astype(F32)

time: 65.7 us -> 65.5 us (level)
  no operation moved by 1% of the time
where the time goes in v7:
time: 65.5 us; the launch traced here: 65.4 us
  Pallas kernels  64.1 us (98%)
  between operations  1.29 us (2%)
    pallas_call x1, Pallas kernels, local(): pl.pallas_call(step_kernel, out_shape=(jax.ShapeDtypeStruct((8, ATOMS), F...  61.9 us
    pallas_call x1, Pallas kernels, local(): pl.pallas_call(finish_kernel, out_shape=(jax.ShapeDtypeStruct((3, ATOMS),...  2.2 us

profile of v7, /device:TPU:1, one launch (start us, length us, event | category | flops | bytes accessed | tf_op | source)
XLA Modules:
  0.0 65.4 jit_solution(4172443391884773251)
XLA Ops:
  1.3 61.9 %step.1 = (f32[8,2048]{1,0:T(8,128)}, bf16[128,2048]{1,0:T(8,128)(2,1)}) custom-call(s32[1,512]{1,0:T(1,128)} %row_ids.1, s32[16,2048]{1,0:T(8,128)} %slots.1, s32[1,2048]{1,0:T(1,128)} %bitcast.2, f32[3,2048]{1,0:T(4,128)} %fractions.1, s32[1]{0:T(128)S(6)} %copy.13.atom_count, bf16[2048,128]{1,0:T(8,128)(2,1)} %features.1, bf16[128,128]{1,0:T(8,128)(2,1)} %w_in.3, ...), custom_call_target="tpu_custom_call" | custom-call | tf_op jit(solution)/shard_map/step/pallas_call | solution.py:643
  63.2 2.2 %finish.1 = (f32[3,2048]{1,0:T(4,128)}, bf16[2048,128]{1,0:T(8,128)(2,1)}) custom-call(f32[8,2048]{1,0:T(8,128)} %get-tuple-element.4.sums, bf16[128,2048]{1,0:T(8,128)(2,1)} %get-tuple-element.5.lifts, bf16[128,128]{1,0:T(8,128)(2,1)} %w_in.3), custom_call_target="tpu_custom_call" | custom-call | tf_op jit(solution)/shard_map/finish/pallas_call | solution.py:712

commit v8 on v6

--- a/solution.py
+++ b/solution.py
@@ -477,21 +477,25 @@
             bins = slice(c * 128, (c + 1) * 128)
             replies[half, :, bins] = jnp.transpose(replies_t[half, bins, :])
         if half == 0:
-            pltpu.make_async_copy(own, returned.at[core * 128 + low], recv_two).start()
+            pltpu.make_async_copy(own, returned.at[core * 128 + low], recv_two.at[0]).start()
             pltpu.make_async_copy(own, spare_two, send_two).start()
         send_half(
             half,
             lambda there: replies.at[half, place_of(there[0], there[1], there[2], 0)],
             returned.at[core * 128 + low],
             send_two,
-            recv_two,
+            recv_two.at[half],
         )
     await_bytes(sent, send_one)
-    await_bytes(returned, recv_two)
-
-    field_high[...], field_low[...] = split(
-        dot3((basis_t[0], basis_t[1]), split(returned[...]))
-    )
+
+    for half in range(2):
+        at = pl.ds(pl.multiple_of(lax.rem(core + half, 2) * 128, 128), 128)
+        await_bytes(returned.at[at], recv_two.at[half])
+        part = dot3((basis_t[0, :, at], basis_t[1, :, at]), split(returned[at, :]))
+        if half == 0:
+            mesh_rows[...] = part
+        else:
+            field_high[...], field_low[...] = split(mesh_rows[...] + part)
     for c in range(ATOMS // CHUNK):
         lanes = slice(c * CHUNK, (c + 1) * CHUNK)
         key = tab_z[8:16, lanes]
@@ -675,7 +679,7 @@
             pltpu.SemaphoreType.DMA,
             pltpu.SemaphoreType.DMA((2,)),
             pltpu.SemaphoreType.DMA,
-            pltpu.SemaphoreType.DMA,
+            pltpu.SemaphoreType.DMA((2,)),
         ],
         compiler_params=pltpu.CompilerParams(
             vmem_limit_bytes=VMEM_LIMIT, collective_id=0, has_side_effects=True

time: 65.7 us -> 65.7 us (level)
  no operation moved by 1% of the time
where the time goes in v8:
time: 65.7 us; the launch traced here: 65.5 us
  Pallas kernels  64.3 us (98%)
  between operations  1.29 us (2%)
    pallas_call x1, Pallas kernels, local(): pl.pallas_call(step_kernel, out_shape=(jax.ShapeDtypeStruct((8, ATOMS), F...  62.1 us
    pallas_call x1, Pallas kernels, local(): pl.pallas_call(finish_kernel, out_shape=(jax.ShapeDtypeStruct((3, ATOMS),...  2.19 us

profile of v8, /device:TPU:1, one launch (start us, length us, event | category | flops | bytes accessed | tf_op | source)
XLA Modules:
  0.0 65.5 jit_solution(7959710821310870973)
XLA Ops:
  1.3 62.1 %step.1 = (f32[8,2048]{1,0:T(8,128)}, bf16[128,2048]{1,0:T(8,128)(2,1)}) custom-call(s32[1,512]{1,0:T(1,128)} %row_ids.1, s32[16,2048]{1,0:T(8,128)} %slots.1, s32[1,2048]{1,0:T(1,128)} %bitcast.2, f32[3,2048]{1,0:T(4,128)} %fractions.1, s32[1]{0:T(128)S(6)} %copy.13.atom_count, bf16[2048,128]{1,0:T(8,128)(2,1)} %features.1, bf16[128,128]{1,0:T(8,128)(2,1)} %w_in.3, ...), custom_call_target="tpu_custom_call" | custom-call | tf_op jit(solution)/shard_map/step/pallas_call | solution.py:632
  63.3 2.2 %finish.1 = (f32[3,2048]{1,0:T(4,128)}, bf16[2048,128]{1,0:T(8,128)(2,1)}) custom-call(f32[8,2048]{1,0:T(8,128)} %get-tuple-element.4.sums, bf16[128,2048]{1,0:T(8,128)(2,1)} %get-tuple-element.5.lifts, bf16[128,128]{1,0:T(8,128)(2,1)} %w_in.3), custom_call_target="tpu_custom_call" | custom-call | tf_op jit(solution)/shard_map/finish/pallas_call | solution.py:701
